TPU v7x, 32 devices: a whole 2x2x4 slice. The times are simulated.
32 devices in a mesh: parts: 2 (over x), row: 16 (over z, y, core).
Axes of the slice: x: 2, y: 2, z: 4, core: 2. Of those that a mesh axis runs over, the one named last changes fastest.
Arguments:
- features: bfloat16 [8192, 256], P(('parts', 'row')), parts along dimension 0, may hold values from -6 to 6
- weight: bfloat16 [256, 256], replicated, may hold values from -0.375 to 0.375
- bias: float32 [256], replicated, may hold values from -3 to 3
- tiles: bfloat16 [2048, 256, 256], P(('parts', 'row')), parts along dimension 0, may hold values from -0.15625 to 0.15625
- tile_col: int32 [32, 64], P(('parts', 'row')), parts along dimension 0, may hold values from 0 to 15
- live_tiles: int32 [32], P(('parts', 'row')), parts along dimension 0, may hold values from 1 to 64, 512 in all
- cotangent: bfloat16 [8192, 256], P(('parts', 'row')), parts along dimension 0, may hold values from -6 to 6
Outputs:
- activation: bfloat16 [8192, 256], P(('parts', 'row')), parts along dimension 0
- grad_features: bfloat16 [8192, 256], P(('parts', 'row')), parts along dimension 0
- grad_weight: float32 [512, 256], P('parts'), parts along dimension 0
- grad_bias: float32 [512], P('parts'), parts along dimension 0
There are 2 independent parts, one for each index of `parts`. A program takes and returns all parts, laid end to end along the dimension named above; an argument that names none is the same for every part. Nothing has to cross between parts.
Inputs may be any that keep to these rules, and one draw needn't show every extreme that they name: `live_tiles`: the counts sum to 16 * 32 and one block row reaches 64.
All inputs are finite; a program needn't handle non-finite values.
Results may differ from a plain program's by a relative error of at most 0.007.
Values may be sent and summed in bfloat16 or wider, within the bound.
No kernel may reach another device: no remote copies, remote signals or barrier semaphores. Data moves between devices by JAX's collectives and lax.ppermute only.
A program may use at most 128 MiB of HBM per device.

v0:
```python
import jax
import jax.numpy as jnp
from jax import lax
from jax.sharding import PartitionSpec as P


def on_device(features, weight, bias, tiles, tile_col, live_tiles, cotangent):
    tile_side = tiles.shape[1]
    slots = tiles.shape[0]
    width = weight.shape[1]
    block_count = lax.axis_size("row")
    columns = tile_col[0]
    slot_ids = jnp.arange(slots, dtype=jnp.int32)
    alive = slot_ids < live_tiles[0]
    same = columns[:, None] == columns[None, :]
    earlier = slot_ids[None, :] < slot_ids[:, None]
    repeated = jnp.any(same & earlier & alive[None, :], axis=1)
    first = alive & jnp.logical_not(repeated)
    merge = (same & first[:, None] & alive[None, :]).astype(jnp.bfloat16)
    compact = jnp.einsum("st,tab->sab", merge, tiles, preferred_element_type=jnp.float32).astype(
        jnp.bfloat16
    )
    projected = jnp.dot(features, weight, preferred_element_type=jnp.float32).astype(jnp.bfloat16)
    gathered = lax.all_gather(projected, "row", axis=0, tiled=True).reshape(-1, tile_side, width)
    chosen = gathered[columns]
    aggregate = jnp.einsum("sab,sbf->af", compact, chosen, preferred_element_type=jnp.float32)
    pre = aggregate + bias[None, :]
    sigma = jax.nn.sigmoid(pre)
    activation = (pre * sigma).astype(jnp.bfloat16)
    grad_pre = (cotangent.astype(jnp.float32) * sigma * (1.0 + pre * (1.0 - sigma))).astype(
        jnp.bfloat16
    )
    block_ids = jnp.arange(block_count, dtype=jnp.int32)
    owner_match = (block_ids[:, None] == columns[None, :]) & first[None, :]
    contrib = jnp.einsum("sab,af->sbf", compact, grad_pre, preferred_element_type=jnp.float32)
    padded = jnp.concatenate([contrib, jnp.zeros((1, tile_side, width), jnp.float32)], axis=0)
    has_owner = jnp.any(owner_match, axis=1)
    owner_slot = jnp.sum(owner_match.astype(jnp.int32) * slot_ids[None, :], axis=1)
    owner = jnp.where(has_owner, owner_slot, slots)
    grad_projected = lax.psum_scatter(
        padded[owner].reshape(tile_side * lax.axis_size("row"), width),
        "row",
        scatter_dimension=0,
        tiled=True,
    ).astype(jnp.bfloat16)
    local_weight = lax.dot_general(
        features, grad_projected, (((0,), (0,)), ((), ())), preferred_element_type=jnp.float32
    )
    local_bias = jnp.sum(grad_pre.astype(jnp.float32), axis=0)
    grad_weight, grad_bias = lax.psum((local_weight, local_bias), "row")
    grad_features = lax.dot_general(
        grad_projected, weight, (((1,), (1,)), ((), ())), preferred_element_type=jnp.float32
    ).astype(jnp.bfloat16)
    return (activation, grad_features, grad_weight, grad_bias)


def solution(mesh):
    placed = (
        P(("parts", "row"), None),
        P(),
        P(),
        P(("parts", "row"), None, None),
        P(("parts", "row"), None),
        P(("parts", "row")),
        P(("parts", "row"), None),
    )
    return jax.shard_map(
        on_device,
        mesh=mesh,
        in_specs=placed,
        out_specs=(
            P(("parts", "row"), None),
            P(("parts", "row"), None),
            P("parts", None),
            P("parts"),
        ),
        check_vma=False,
    )
```

profile of v0, /device:TPU:0, one launch (start us, length us, event | category | flops | bytes accessed | tf_op | source)
XLA Modules:
  0.0 263.2 jit_solution(2809509626498781449)
XLA Ops:
  7.2 0.0 copy-start
  7.2 0.0 all-gather.2.cloned.1.call-start
  7.2 0.8 copy-done
  8.1 1.7 convolution_convert_fusion.1
  9.8 0.0 all-gather.2.cloned.1.call-update
  9.8 0.0 reduce-scatter.2.cloned.1.call-start
  10.6 0.9 fusion.11
  11.5 13.1 %fusion.2 = bf16[64,256,256]{2,0,1:T(8,128)(2,1)} fusion(bf16[64,256,256]{2,1,0:T(8,128)(2,1)} %param.10, s32[64]{0:T(128)} %bitcast.36, pred[64]{0:T(512)(128)(4,1)S(1)} %not_and_fusion, pred[64]{0:T(512)(128)(4,1)S(1)} %iota_compare_fusion.2), kind=kOutput, calls=%fused_computation.4 | convolution fusion | flops 541077504 | bytes 16777600 | tf_op jit(solution)/shard_map/st,tab->sab/dot_general | solution.py:20
  24.6 0.0 copy-start.3
  24.6 12.9 %copy.17 = bf16[64,256,256]{1,2,0:T(8,128)(2,1)} copy(bf16[64,256,256]{2,0,1:T(8,128)(2,1)} %fusion.2) | data formatting | bytes 16777216 | tf_op jit(solution)/shard_map/convert_element_type | solution.py:20
  37.4 0.0 copy-done.3
  37.5 0.1 fusion.20
  37.6 0.1 select_reduce_fusion
  37.7 17.2 %all-gather.2.cloned.1.call-done = bf16[4096,256]{1,0:T(8,128)(2,1)} async-done(((bf16[256,256]{1,0:T(8,128)(2,1)}), bf16[4096,256]{1,0:T(8,128)(2,1)}) %all-gather.2.cloned.1.call-update) | async-done | bytes 2097168 | tf_op jit(solution)/shard_map/all_gather | solution.py:24
  54.9 0.0 copy-start.2
  54.9 0.0 copy-start.4
  54.9 7.1 %gather_fusion = bf16[64,256,256]{2,1,0:T(8,128)(2,1)} fusion(bf16[16,256,256]{2,1,0:T(8,128)(2,1)} %bitcast.33, s32[1024]{0:T(1024)S(1)} %pad_clamp_fusion.1), kind=kCustom, calls=%fused_computation | custom fusion | bytes 16777472 | tf_op jit(solution)/shard_map/gather | solution.py:25
  62.0 0.0 copy-done.2
  62.0 0.0 copy-done.4
  62.0 8.9 %convert_reduce_fusion = (f32[256]{0:T(256)S(1)}, bf16[256,256]{1,0:T(8,128)(2,1)S(1)}, bf16[256,256]{1,0:T(8,128)(2,1)}) fusion(bf16[256,256]{1,0:T(8,128)(2,1)S(1)} %copy-done.2, f32[256]{0:T(256)S(1)} %copy-done.4, bf16[64,256,256]{1,2,0:T(8,128)(2,1)} %copy.17, bf16[64,256,256]{2,1,0:T(8,128)(2,1)} %gather_fusion), kind=kOutput, calls=%fused_computation.10 | convolution fusion | flops 2148466432 | bytes 17172480 | tf_op jit(solution)/shard_map/sab,sbf->af/dot_general | solution.py:26
  70.9 5.7 %fusion.6 = f32[64,256,256]{2,1,0:T(8,128)S(1)} fusion(bf16[64,256,256]{1,2,0:T(8,128)(2,1)} %copy.17, bf16[256,256]{1,0:T(8,128)(2,1)S(1)} %get-tuple-element.13), kind=kOutput, calls=%fused_computation.14 | convolution fusion | flops 2147483648 | bytes 25296896 | tf_op jit(solution)/shard_map/sab,af->sbf/dot_general | solution.py:35
  76.6 6.1 %concatenate.3 = f32[65,256,256]{2,1,0:T(8,128)} pad(f32[64,256,256]{2,1,0:T(8,128)S(1)} %fusion.6, f32[]{:T(128)} %constant.2.clone.1), padding=0_1x0_0x0_0 | pad | bytes 33816580 | tf_op jit(solution)/shard_map/concatenate | solution.py:36
  82.7 0.0 copy-start.1
  82.7 8.6 %gather_fusion.1 = f32[16,256,256]{2,1,0:T(8,128)} fusion(f32[65,256,256]{2,1,0:T(8,128)} %concatenate.3, s32[1024]{0:T(1024)S(1)} %pad_clamp_fusion), kind=kCustom, calls=%fused_computation.1 | custom fusion | bytes 8388672 | tf_op jit(solution)/shard_map/gather | solution.py:41
  91.4 0.0 reduce-scatter.2.cloned.1.call-update
  91.4 0.0 all-reduce.3.cloned.1.call-start
  91.4 32.1 %psum.15 = f32[256]{0:T(256)} all-reduce(f32[256]{0:T(256)S(1)} %get-tuple-element.12), channel_id=1, replica_groups=mesh['parts'=2,'row'=16] {'row'}, use_global_device_ids=true, to_apply=%region_6.7 | all-reduce | flops 256 | bytes 2048 | tf_op jit(solution)/shard_map/psum | solution.py:50
  123.5 39.3 %reduce-scatter.2.cloned.1.call-done = f32[256,256]{1,0:T(8,128)} async-done(((f32[4096,256]{1,0:T(8,128)}), f32[256,256]{1,0:T(8,128)}) %reduce-scatter.2.cloned.1.call-update) | async-done | bytes 262160 | tf_op jit(solution)/shard_map/reduce_scatter | solution.py:40
  162.8 1.9 convolution_bitcast_fusion
  164.7 0.0 all-reduce.3.cloned.1.call-update
  164.7 0.0 copy-done.1
  164.7 1.8 convolution_convert_fusion
  166.5 88.4 %all-reduce.3.cloned.1.call-done = f32[256,256]{0,1:T(8,128)} async-done(((f32[256,256]{0,1:T(8,128)}), f32[256,256]{0,1:T(8,128)}) %all-reduce.3.cloned.1.call-update) | async-done | bytes 262160 | tf_op jit(solution)/shard_map/psum | solution.py:50
  254.9 1.8 copy.18
  (6 shorter events, 0.0 us)
Async XLA Ops:
  7.2 0.9 copy-start
  7.2 47.7 %all-gather.2.cloned.1.call-start = ((), (), s32[]{:S(2)}) async-start(), calls=%async_computation.1 | async-start | bytes 2228224 | tf_op jit(solution)/shard_map/all_gather | solution.py:24
  9.8 152.9 %reduce-scatter.2.cloned.1.call-start = ((), (), s32[]{:S(2)}) async-start(), calls=%async_computation.2 | async-start | bytes 4456448 | tf_op jit(solution)/shard_map/reduce_scatter | solution.py:40
  24.6 12.9 %copy-start.3 = (s32[1,64]{1,0:T(1,128)S(1)}, s32[1,64]{1,0:T(1,128)}, u32[]{:S(2)}) copy-start(s32[1,64]{1,0:T(1,128)} %param.11) | copy-start | bytes 772
  54.9 7.1 %copy-start.2 = (bf16[256,256]{1,0:T(8,128)(2,1)S(1)}, bf16[256,256]{1,0:T(8,128)(2,1)}, u32[]{:S(2)}) copy-start(bf16[256,256]{1,0:T(8,128)(2,1)} %param.13) | copy-start | bytes 393220
  54.9 7.1 %copy-start.4 = (f32[256]{0:T(256)S(1)}, f32[256]{0:T(256)}, u32[]{:S(2)}) copy-start(f32[256]{0:T(256)} %param.9) | copy-start | bytes 3076
  82.7 82.0 %copy-start.1 = (bf16[256,256]{1,0:T(8,128)(2,1)S(1)}, bf16[256,256]{1,0:T(8,128)(2,1)}, u32[]{:S(2)}) copy-start(bf16[256,256]{1,0:T(8,128)(2,1)} %param.8) | copy-start | bytes 393220
  91.4 163.5 %all-reduce.3.cloned.1.call-start = ((), (), s32[]{:S(2)}) async-start(), calls=%async_computation.3 | async-start | bytes 524288 | tf_op jit(solution)/shard_map/psum | solution.py:50
Sparse Core Ops, SparseCore 0:
  10.7 44.0 all-gather.1
  91.5 71.2 reduce-scatter.1
  167.1 87.7 all-reduce.2
where the time goes:
time: 264 us; the launch traced here: 263 us
  waiting for transfers between devices  145 us (55%)
  local copies, waits for them, and re-layouts  37.4 us (14%)
  matrix products  33.1 us (13%)
  blocking collectives  32.1 us (12%)
  between operations  14.4 us (5%)
    psum x1, waiting for transfers between devices, on_device(): grad_weight, grad_bias = lax.psum((local_weight, local_bias), 'row')  88.4 us
    reduce_scatter x1, waiting for transfers between devices, on_device(): lax.psum_scatter(padded[owner].reshape(tile_side * lax.axis_size('row'),...  39.3 us
    psum x1, blocking collectives, on_device(): grad_weight, grad_bias = lax.psum((local_weight, local_bias), 'row')  32.1 us
    all_gather x1, waiting for transfers between devices, on_device(): lax.all_gather(projected, 'row', axis=0, tiled=True)  17.2 us
    dot_general x1, matrix products, on_device(): jnp.einsum('st,tab->sab', merge, tiles, preferred_element_type=jnp.float32)  13.1 us
    convert_element_type x1, local copies, waits for them, and re-layouts, on_device(): jnp.einsum('st,tab->sab', merge, tiles, preferred_element_type=jnp.float32)  12.9 us
    dot_general x1, matrix products, on_device(): jnp.einsum('sab,sbf->af', compact, chosen, preferred_element_type=jnp.flo...  8.88 us
    gather x1, local copies, waits for them, and re-layouts, on_device(): padded[owner].reshape(tile_side * lax.axis_size('row'), width)  8.64 us
  transfers between devices with their start and end apart: 3, of which 3 were waited for; matrix products, arithmetic and copies ran while one was open for 11% of the time, Pallas kernels for 0%

commit v1 on v0

v1 whole, which is shorter than its diff:
```python
import functools

import jax
import jax.numpy as jnp
from jax import lax
from jax.experimental import pallas as pl
from jax.experimental.pallas import tpu as pltpu
from jax.sharding import PartitionSpec as P

F32 = jnp.float32
BF16 = jnp.bfloat16
VMEM = pl.BlockSpec(memory_space=pltpu.VMEM)
SMEM = pl.BlockSpec(memory_space=pltpu.SMEM)
LIMIT = 48 * 1024 * 1024


def dot(a, b):
    return jnp.dot(a, b, preferred_element_type=F32)


def halves(x):
    high = x.astype(BF16)
    return high, (x - high.astype(F32)).astype(BF16)


def call(kernel, out_shape, args, in_specs=None, scratch=(), flops=0, moved=0):
    many = isinstance(out_shape, (list, tuple))
    return pl.pallas_call(
        kernel,
        out_shape=out_shape,
        in_specs=in_specs or [VMEM] * len(args),
        out_specs=[VMEM] * len(out_shape) if many else VMEM,
        scratch_shapes=list(scratch),
        compiler_params=pltpu.CompilerParams(vmem_limit_bytes=LIMIT),
        cost_estimate=pl.CostEstimate(flops=flops, bytes_accessed=moved, transcendentals=0),
    )(*args)


def merge_kernel(columns, live, me, tiles, own, other, held, total, sems):
    count = live[0]
    blocks = total.shape[0]

    def fetch(slot):
        return pltpu.make_async_copy(tiles.at[slot], held.at[slot], sems.at[slot])

    def start(slot, carry):
        fetch(slot).start()
        return carry

    lax.fori_loop(0, count, start, 0)

    def clear(index, carry):
        total[index] = jnp.zeros(total.shape[1:], F32)
        return carry

    lax.fori_loop(0, blocks, clear, 0)

    def add(slot, carry):
        fetch(slot).wait()
        where = lax.bitwise_xor(columns[slot], me[0])
        total[where] += held[slot].astype(F32)
        return carry

    lax.fori_loop(0, count, add, 0)

    def store(index, carry):
        own[index] = total[2 * index].astype(BF16)
        other[index] = total[2 * index + 1].astype(BF16)
        return carry

    lax.fori_loop(0, blocks // 2, store, 0)


def aggregate_kernel(own, other, *refs):
    xs, (mine, partner) = refs[:-2], refs[-2:]
    total_mine = jnp.zeros(mine.shape, F32)
    total_partner = jnp.zeros(mine.shape, F32)
    for index, x in enumerate(xs):
        total_mine += dot(own[index], x[...])
        total_partner += dot(other[index], x[...])
    mine[...] = total_mine
    partner[...] = total_partner


def layer_kernel(mine, received, weight, bias, cotangent, activation, grad_pre_t, grad_bias):
    high, low = halves(mine[...] + received[...])
    pre = dot(high, weight[...]) + dot(low, weight[...]) + bias[...]
    sigma = jax.nn.sigmoid(pre)
    activation[...] = (pre * sigma).astype(BF16)
    grad = (cotangent[...].astype(F32) * sigma * (1.0 + pre * (1.0 - sigma))).astype(BF16)
    grad = grad.astype(F32)
    grad_bias[...] = jnp.broadcast_to(jnp.sum(grad, axis=0, keepdims=True), grad_bias.shape)
    grad_pre_t[...] = grad.T.astype(BF16)


def backward_kernel(groups, core, own, other, grad, grad_other, mine, partner, grad_bias, *refs):
    sends, (keep, weight_keep, weight_send, whole) = refs[:len(groups)], refs[len(groups):]
    g, go = grad[...], grad_other[...]
    place = 0
    for send, group in zip(sends, groups):
        for slot, z in enumerate(group):
            at = z // 2
            send[slot] = (dot(g, own[at + 1]) + dot(go, other[at + 1])).astype(BF16)
            keep[place] = dot(g, own[at]) + dot(go, other[at])
            place += 1
    high, low = halves(mine[...])
    high_o, low_o = halves(partner[...])
    whole[...] = (dot(g, high) + dot(g, low) + dot(go, high_o) + dot(go, low_o)).T
    half = weight_keep.shape[0] - 8
    for out, which in ((weight_keep, core[0]), (weight_send, 1 - core[0])):
        out[pl.ds(0, half), :] = whole[pl.ds(pl.multiple_of(which * half, half), half), :]
        out[pl.ds(half, 8), :] = grad_bias[...]


def finish_kernel(kept, from_y, *refs):
    arrived, (weight, grad_features) = refs[:-2], refs[-2:]
    total = kept[...] + from_y[...].astype(F32)
    for part in arrived:
        total += part[...].astype(F32)
    grad_features[...] = lax.dot_general(
        total.T.astype(BF16), weight[...], (((1,), (1,)), ((), ())), preferred_element_type=F32
    ).astype(BF16)


def on_device(features, weight, bias, tiles, tile_col, live_tiles, cotangent):
    side, width = features.shape
    slots = tiles.shape[0]
    count = lax.axis_size("row")
    pairs = count // 2
    me = lax.axis_index("row").astype(jnp.int32)
    core = jnp.bitwise_and(me, 1)

    def swap(x, bit):
        return lax.ppermute(x, "row", [(i, i ^ bit) for i in range(count)])

    block = (side, width)
    own, send_other = call(
        merge_kernel,
        [jax.ShapeDtypeStruct((pairs, side, side), BF16)] * 2,
        (tile_col[0], live_tiles, me[None], tiles),
        in_specs=[SMEM, SMEM, SMEM, pl.BlockSpec(memory_space=pl.ANY)],
        scratch=[
            pltpu.VMEM((slots, side, side), BF16),
            pltpu.VMEM((count, side, side), F32),
            pltpu.SemaphoreType.DMA((slots,)),
        ],
        flops=slots * side * side,
        moved=slots * side * side * 2,
    )
    zs = list(range(count - 4, -4, -4))
    gathered = {0: features}
    for z in zs[:-1]:
        gathered[z] = swap(features, z)
    gathered[2] = swap(features, 2)
    for z in reversed(zs[:-1]):
        gathered[z + 2] = swap(gathered[z], 2)
    other = swap(send_other, 1)
    xs = [gathered[2 * index] for index in range(pairs)]
    mine, partner = call(
        aggregate_kernel,
        [jax.ShapeDtypeStruct(block, F32)] * 2,
        (own, other, *xs),
        flops=4 * pairs * side**2 * width,
        moved=3 * pairs * side * width * 2,
    )
    received = swap(partner, 1)
    activation, grad, grad_bias = call(
        layer_kernel,
        [
            jax.ShapeDtypeStruct(block, BF16),
            jax.ShapeDtypeStruct((width, side), BF16),
            jax.ShapeDtypeStruct((8, width), F32),
        ],
        (mine, received, weight, bias[None, :], cotangent),
        flops=4 * side * width**2,
        moved=side * width * 16,
    )
    grad_other = swap(grad, 1)
    middle = (len(zs) + 1) // 2
    groups = [zs[:middle], zs[middle:]]
    half = jax.ShapeDtypeStruct((width // 2 + 8, width), F32)
    *sends, keep, weight_keep, weight_send = call(
        functools.partial(backward_kernel, groups),
        [jax.ShapeDtypeStruct((len(group), width, side), BF16) for group in groups]
        + [jax.ShapeDtypeStruct((len(zs), width, side), F32), half, half],
        (core[None], own, other, grad, grad_other, mine, partner, grad_bias),
        in_specs=[SMEM] + [VMEM] * 7,
        scratch=[pltpu.VMEM((width, width), F32)],
        flops=4 * pairs * side**2 * width,
        moved=3 * pairs * side * width * 2,
    )
    arrived = []
    place = 0
    from_y = [swap(send, 2) for send in sends]
    for group, received_y in zip(groups, from_y):
        for slot, z in enumerate(group):
            if z:
                summed = (keep[place] + received_y[slot].astype(F32)).astype(BF16)
                arrived.append(swap(summed, z))
            place += 1
    part = weight_keep + swap(weight_send, 1)
    bit = 2
    while bit < count:
        part = part + swap(part, bit)
        bit *= 2
    mine_w = part[: width // 2]
    other_w = swap(mine_w, 1)
    grad_weight = jnp.where(
        core == 0, jnp.concatenate([mine_w, other_w]), jnp.concatenate([other_w, mine_w])
    )
    grad_features = call(
        finish_kernel,
        jax.ShapeDtypeStruct(block, BF16),
        (keep[-1], from_y[-1][-1], *arrived, weight),
        flops=2 * side * width**2,
        moved=side * width * 2 * (len(zs) + 4),
    )
    return activation, grad_features, grad_weight, part[width // 2]


def solution(mesh):
    placed = (
        P(("parts", "row"), None),
        P(),
        P(),
        P(("parts", "row"), None, None),
        P(("parts", "row"), None),
        P(("parts", "row")),
        P(("parts", "row"), None),
    )
    return jax.shard_map(
        on_device,
        mesh=mesh,
        in_specs=placed,
        out_specs=(
            P(("parts", "row"), None),
            P(("parts", "row"), None),
            P("parts", None),
            P("parts"),
        ),
        check_vma=False,
    )
```

time: 264 us -> 73.7 us (0.28)
  waiting for transfers between devices: 145 us -> 27 us
  matrix products: 33.1 us -> 0 us
  local copies, waits for them, and re-layouts: 37.4 us -> 5.3 us
  blocking collectives: 32.1 us -> 0 us
  starting transfers between devices: 0.12 us -> 31.7 us
  between operations: 14.4 us -> 1.47 us
  Pallas kernels: 0 us -> 7.28 us
    psum x1 -> x0, waiting for transfers between devices: 88.4 us -> none  [on_device(): grad_weight, grad_bias = lax.psum((local_weight, local_bias), 'row')]
    reduce_scatter x1 -> x0, waiting for transfers between devices: 39.3 us -> none  [on_device(): lax.psum_scatter(padded[owner].reshape(tile_side * lax.axis_size('row'),...]
    dot_general x6 -> x0, matrix products: 33.1 us -> none  [the longest x1 13.1 us: on_device(): jnp.einsum('st,tab->sab', merge, tiles, preferred_element_type=jnp.float32)]
    psum x1 -> x0, blocking collectives: 32.1 us -> none  [on_device(): grad_weight, grad_bias = lax.psum((local_weight, local_bias), 'row')]
    ppermute x0 -> x20, starting transfers between devices: none -> 31.7 us  [swap(): return lax.ppermute(x, 'row', [(i, i ^ bit) for i in range(count)])]
    ppermute x0 -> x20, waiting for transfers between devices: none -> 27 us  [swap(): return lax.ppermute(x, 'row', [(i, i ^ bit) for i in range(count)])]
    all_gather x1 -> x0, waiting for transfers between devices: 17.2 us -> none  [on_device(): lax.all_gather(projected, 'row', axis=0, tiled=True)]
    gather x2 -> x0, local copies, waits for them, and re-layouts: 15.8 us -> none  [the longest x1 8.64 us: on_device(): padded[owner].reshape(tile_side * lax.axis_size('row'), width)]
  transfers between devices with their start and end apart: 3 -> 20, of which waited for: 3 -> 11; matrix products, arithmetic and copies ran while one was open for 11% -> 1% of each run, Pallas kernels for 0% -> 1%
where the time goes in v1:
time: 73.7 us
  starting transfers between devices  31.7 us (43%)
  waiting for transfers between devices  27 us (37%)
  Pallas kernels  7.28 us (10%)
  local copies, waits for them, and re-layouts  5.3 us (7%)
  between operations  1.47 us (2%)
  other arithmetic  0.96 us (1%)
    ppermute x20, starting transfers between devices, swap(): return lax.ppermute(x, 'row', [(i, i ^ bit) for i in range(count)])  31.7 us
    ppermute x20, waiting for transfers between devices, swap(): return lax.ppermute(x, 'row', [(i, i ^ bit) for i in range(count)])  27 us
    pallas_call x5, Pallas kernels, call(): pl.pallas_call(kernel, out_shape=out_shape, in_specs=in_specs or [VMEM] *...  7.28 us
    unnamed x22, local copies, waits for them, and re-layouts  4.72 us
  transfers between devices with their start and end apart: 20, of which 11 were waited for; matrix products, arithmetic and copies ran while one was open for 1% of the time, Pallas kernels for 1%

profile of v1, /device:TPU:0, one launch (start us, length us, event | category | flops | bytes accessed | tf_op | source)
XLA Modules:
  0.0 73.7 jit_solution(12364200809304348977)
XLA Ops:
  1.4 0.6 copy-done.10
  2.0 3.1 %shard_map.102 = (bf16[8,256,256]{2,1,0:T(8,128)(2,1)S(1)}, bf16[8,256,256]{2,1,0:T(8,128)(2,1)S(1)}) custom-call(s32[64]{0:T(128)S(1)} %bitcast.16, s32[1]{0:T(128)S(6)} %copy.11.live, s32[1]{0:T(128)} %bitcast.1.me, bf16[64,256,256]{2,1,0:T(8,128)(2,1)} %tiles.1), custom_call_target="tpu_custom_call" | custom-call | flops 4194304 | bytes 8388608 | tf_op jit(solution)/shard_map/pallas_call | solution.py:28
  5.1 2.3 %collective-permute-start = (bf16[8,256,256]{2,1,0:T(8,128)(2,1)S(1)}, bf16[8,256,256]{2,1,0:T(8,128)(2,1)S(1)}, u32[]{:S(2)}, u32[]{:S(2)}) collective-permute-start(bf16[8,256,256]{2,1,0:T(8,128)(2,1)S(1)} %get-tuple-element.17), channel_id=1, source_target_pairs={{0,1},{1,0},{2,3},{3,2},{4,5},{5,4},{6,7},{7,6},{8,9},{9,8},{10,11... | collective-permute-start | bytes 3145736 | tf_op jit(solution)/shard_map/ppermute | solution.py:134
  7.4 1.4 %collective-permute-start.2 = (bf16[256,256]{1,0:T(8,128)(2,1)S(1)}, bf16[256,256]{1,0:T(8,128)(2,1)S(1)}, u32[]{:S(2)}, u32[]{:S(2)}) collective-permute-start(bf16[256,256]{1,0:T(8,128)(2,1)S(1)} %copy-done.3), channel_id=1, source_target_pairs={{0,4},{1,5},{2,6},{3,7},{4,0},{5,1},{6,2},{7,3},{8,12},{9,13},{10,... | collective-permute-start | bytes 393224 | tf_op jit(solution)/shard_map/ppermute | solution.py:134
  8.8 2.5 %collective-permute-start.4 = (bf16[256,256]{1,0:T(8,128)(2,1)S(1)}, bf16[256,256]{1,0:T(8,128)(2,1)S(1)}, u32[]{:S(2)}, u32[]{:S(2)}) collective-permute-start(bf16[256,256]{1,0:T(8,128)(2,1)S(1)} %copy-done.3), channel_id=1, source_target_pairs={{0,8},{1,9},{2,10},{3,11},{4,12},{5,13},{6,14},{7,15},{8,0},{9,1},... | collective-permute-start | bytes 393224 | tf_op jit(solution)/shard_map/ppermute | solution.py:134
  11.3 1.0 %collective-permute-start.6 = (bf16[256,256]{1,0:T(8,128)(2,1)S(1)}, bf16[256,256]{1,0:T(8,128)(2,1)S(1)}, u32[]{:S(2)}, u32[]{:S(2)}) collective-permute-start(bf16[256,256]{1,0:T(8,128)(2,1)S(1)} %copy-done.3), channel_id=1, source_target_pairs={{0,12},{1,13},{2,14},{3,15},{4,8},{5,9},{6,10},{7,11},{8,4},{9,5},... | collective-permute-start | bytes 393224 | tf_op jit(solution)/shard_map/ppermute | solution.py:134
  12.3 1.9 %collective-permute-start.1 = (bf16[256,256]{1,0:T(8,128)(2,1)S(1)}, bf16[256,256]{1,0:T(8,128)(2,1)S(1)}, u32[]{:S(2)}, u32[]{:S(2)}) collective-permute-start(bf16[256,256]{1,0:T(8,128)(2,1)S(1)} %copy-done.3), channel_id=1, source_target_pairs={{0,2},{1,3},{2,0},{3,1},{4,6},{5,7},{6,4},{7,5},{8,10},{9,11},{10,... | collective-permute-start | bytes 393224 | tf_op jit(solution)/shard_map/ppermute | solution.py:134
  14.2 1.2 %collective-permute-done.2.refs_2_ = bf16[256,256]{1,0:T(8,128)(2,1)S(1)} collective-permute-done((bf16[256,256]{1,0:T(8,128)(2,1)S(1)}, bf16[256,256]{1,0:T(8,128)(2,1)S(1)}, u32[]{:S(2)}, u32[]{:S(2)}) %collective-permute-start.2) | collective-permute-done | bytes 131104 | tf_op jit(solution)/shard_map/ppermute | solution.py:134
  15.4 2.7 %collective-permute-start.3 = (bf16[256,256]{1,0:T(8,128)(2,1)S(1)}, bf16[256,256]{1,0:T(8,128)(2,1)S(1)}, u32[]{:S(2)}, u32[]{:S(2)}) collective-permute-start(bf16[256,256]{1,0:T(8,128)(2,1)S(1)} %collective-permute-done.2.refs_2_), channel_id=1, source_target_pairs={{0,2},{1,3},{2,0},{3,1},{4,6},{5,7},{6,4},{7,5},{8,10},{9,11},{10,... | collective-permute-start | bytes 393224 | tf_op jit(solution)/shard_map/ppermute | solution.py:134
  18.1 0.0 collective-permute-start.5
  18.1 3.3 %collective-permute-done.6.refs_6_ = bf16[256,256]{1,0:T(8,128)(2,1)S(1)} collective-permute-done((bf16[256,256]{1,0:T(8,128)(2,1)S(1)}, bf16[256,256]{1,0:T(8,128)(2,1)S(1)}, u32[]{:S(2)}, u32[]{:S(2)}) %collective-permute-start.6) | collective-permute-done | bytes 131104 | tf_op jit(solution)/shard_map/ppermute | solution.py:134
  21.5 2.2 %collective-permute-start.7 = (bf16[256,256]{1,0:T(8,128)(2,1)S(1)}, bf16[256,256]{1,0:T(8,128)(2,1)S(1)}, u32[]{:S(2)}, u32[]{:S(2)}) collective-permute-start(bf16[256,256]{1,0:T(8,128)(2,1)S(1)} %collective-permute-done.6.refs_6_), channel_id=1, source_target_pairs={{0,2},{1,3},{2,0},{3,1},{4,6},{5,7},{6,4},{7,5},{8,10},{9,11},{10,... | collective-permute-start | bytes 393224 | tf_op jit(solution)/shard_map/ppermute | solution.py:134
  23.6 0.0 collective-permute-done.1.refs_1_
  23.6 0.0 collective-permute-done.3.refs_3_
  23.7 3.2 %collective-permute-done.7.refs_7_ = bf16[256,256]{1,0:T(8,128)(2,1)S(1)} collective-permute-done((bf16[256,256]{1,0:T(8,128)(2,1)S(1)}, bf16[256,256]{1,0:T(8,128)(2,1)S(1)}, u32[]{:S(2)}, u32[]{:S(2)}) %collective-permute-start.7) | collective-permute-done | bytes 131104 | tf_op jit(solution)/shard_map/ppermute | solution.py:134
  26.9 0.7 shard_map.103
  27.6 0.0 copy-start.1
  27.6 0.1 collective-permute-start.8
  27.7 1.5 %collective-permute-done.8.received = f32[256,256]{1,0:T(8,128)S(1)} collective-permute-done((f32[256,256]{1,0:T(8,128)S(1)}, f32[256,256]{1,0:T(8,128)S(1)}, u32[]{:S(2)}, u32[]{:S(2)}) %collective-permute-start.8) | collective-permute-done | bytes 262176 | tf_op jit(solution)/shard_map/ppermute | solution.py:134
  29.2 1.0 %shard_map.104 = (bf16[256,256]{1,0:T(8,128)(2,1)}, bf16[256,256]{1,0:T(8,128)(2,1)S(1)}, f32[8,256]{1,0:T(8,128)S(1)}) custom-call(f32[256,256]{1,0:T(8,128)S(1)} %get-tuple-element.18.mine, f32[256,256]{1,0:T(8,128)S(1)} %collective-permute-done.8.received, bf16[256,256]{1,0:T(8,128)(2,1)S(1)} %copy-done, f32[1,256]{1,0:T(1,128)S(1)} %bitcast.15, ...), custom_call_target="tpu_custom_call" | custom-call | flops 67108864 | bytes 1048576 | tf_op jit(solution)/shard_map/pallas_call | solution.py:28
  30.2 0.1 collective-permute-start.9
  30.3 0.7 copy-done.4
  31.0 0.6 collective-permute-done.9.grad_other
  31.5 0.6 copy-done.6
  32.2 0.9 %copy-done.2 = f32[256,256]{1,0:T(8,128)S(1)} copy-done((f32[256,256]{1,0:T(8,128)S(1)}, f32[256,256]{1,0:T(8,128)}, u32[]{:S(2)}) %copy-start.2) | copy-done | bytes 262168
  33.1 0.9 %copy-done.5 = bf16[256,256]{1,0:T(8,128)(2,1)S(1)} copy-done((bf16[256,256]{1,0:T(8,128)(2,1)S(1)}, bf16[256,256]{1,0:T(8,128)(2,1)}, u32[]{:S(2)}) %copy-start.5) | copy-done | bytes 131096
  34.0 0.9 %copy-done.7 = bf16[256,256]{1,0:T(8,128)(2,1)S(1)} copy-done((bf16[256,256]{1,0:T(8,128)(2,1)S(1)}, bf16[256,256]{1,0:T(8,128)(2,1)}, u32[]{:S(2)}) %copy-start.7) | copy-done | bytes 131096
  34.9 1.6 %shard_map.105 = (bf16[2,256,256]{2,1,0:T(8,128)(2,1)}, bf16[2,256,256]{2,1,0:T(8,128)(2,1)}, f32[4,256,256]{2,1,0:T(8,128)S(1)}, f32[136,256]{1,0:T(8,128)S(1)}, f32[136,256]{1,0:T(8,128)S(1)}) custom-call(s32[1]{0:T(128)} %bitcast.3.core, bf16[8,256,256]{2,1,0:T(8,128)(2,1)S(1)} %get-tuple-element.16.own, ...), custom_call_target="tpu_custom_call" | custom-call | flops 536870912 | bytes 3145728 | tf_op jit(solution)/shard_map/pallas_call | solution.py:28
  36.6 0.1 collective-permute-start.15
  36.7 1.2 %collective-permute-done.15 = f32[136,256]{1,0:T(8,128)S(1)} collective-permute-done((f32[136,256]{1,0:T(8,128)S(1)}, f32[136,256]{1,0:T(8,128)S(1)}, u32[]{:S(2)}, u32[]{:S(2)}) %collective-permute-start.15) | collective-permute-done | bytes 139296 | tf_op jit(solution)/shard_map/ppermute | solution.py:134
  37.9 1.8 %collective-permute-start.16 = (f32[136,256]{1,0:T(8,128)S(1)}, f32[136,256]{1,0:T(8,128)S(1)}, u32[]{:S(2)}, u32[]{:S(2)}) collective-permute-start(f32[136,256]{1,0:T(8,128)S(1)} %add.27), channel_id=1, source_target_pairs={{0,2},{1,3},{2,0},{3,1},{4,6},{5,7},{6,4},{7,5},{8,10},{9,11},{10,... | collective-permute-start | bytes 417800 | tf_op jit(solution)/shard_map/ppermute | solution.py:134
  39.8 0.3 collective-permute-start.11
  40.0 1.7 %collective-permute-start.10 = (bf16[2,256,256]{2,1,0:T(8,128)(2,1)}, bf16[2,256,256]{2,1,0:T(8,128)(2,1)S(1)}, u32[]{:S(2)}, u32[]{:S(2)}) collective-permute-start(bf16[2,256,256]{2,1,0:T(8,128)(2,1)} %get-tuple-element.24), channel_id=1, source_target_pairs={{0,2},{1,3},{2,0},{3,1},{4,6},{5,7},{6,4},{7,5},{8,10},{9,11},{10,... | collective-permute-start | bytes 786440 | tf_op jit(solution)/shard_map/ppermute | solution.py:134
  41.8 2.7 %collective-permute-done.16 = f32[136,256]{1,0:T(8,128)S(1)} collective-permute-done((f32[136,256]{1,0:T(8,128)S(1)}, f32[136,256]{1,0:T(8,128)S(1)}, u32[]{:S(2)}, u32[]{:S(2)}) %collective-permute-start.16) | collective-permute-done | bytes 139296 | tf_op jit(solution)/shard_map/ppermute | solution.py:134
  44.5 3.0 %collective-permute-start.17 = (f32[136,256]{1,0:T(8,128)S(1)}, f32[136,256]{1,0:T(8,128)S(1)}, u32[]{:S(2)}, u32[]{:S(2)}) collective-permute-start(f32[136,256]{1,0:T(8,128)S(1)} %add.28), channel_id=1, source_target_pairs={{0,4},{1,5},{2,6},{3,7},{4,0},{5,1},{6,2},{7,3},{8,12},{9,13},{10,... | collective-permute-start | bytes 417800 | tf_op jit(solution)/shard_map/ppermute | solution.py:134
  47.5 3.0 %collective-permute-done.17 = f32[136,256]{1,0:T(8,128)S(1)} collective-permute-done((f32[136,256]{1,0:T(8,128)S(1)}, f32[136,256]{1,0:T(8,128)S(1)}, u32[]{:S(2)}, u32[]{:S(2)}) %collective-permute-start.17) | collective-permute-done | bytes 139296 | tf_op jit(solution)/shard_map/ppermute | solution.py:134
  50.6 4.0 %collective-permute-start.18 = (f32[136,256]{1,0:T(8,128)S(1)}, f32[136,256]{1,0:T(8,128)S(1)}, u32[]{:S(2)}, u32[]{:S(2)}) collective-permute-start(f32[136,256]{1,0:T(8,128)S(1)} %add.29), channel_id=1, source_target_pairs={{0,8},{1,9},{2,10},{3,11},{4,12},{5,13},{6,14},{7,15},{8,0},{9,1},... | collective-permute-start | bytes 417800 | tf_op jit(solution)/shard_map/ppermute | solution.py:134
  54.6 0.0 collective-permute-done.11
  54.6 0.4 collective-permute-done.10
  55.0 0.1 fusion.1
  55.1 5.8 %collective-permute-start.12 = (bf16[256,256]{1,0:T(8,128)(2,1)S(1)}, bf16[256,256]{1,0:T(8,128)(2,1)S(1)}, u32[]{:S(2)}, u32[]{:S(2)}) collective-permute-start(bf16[256,256]{1,0:T(8,128)(2,1)S(1)} %get-tuple-element.29), channel_id=1, source_target_pairs={{0,12},{1,13},{2,14},{3,15},{4,8},{5,9},{6,10},{7,11},{8,4},{9,5},... | collective-permute-start | bytes 393224 | tf_op jit(solution)/shard_map/ppermute | solution.py:134
  60.9 0.6 collective-permute-start.14
  61.6 0.1 collective-permute-start.19
  61.7 3.7 %collective-permute-done.12.refs_0_ = bf16[256,256]{1,0:T(8,128)(2,1)S(1)} collective-permute-done((bf16[256,256]{1,0:T(8,128)(2,1)S(1)}, bf16[256,256]{1,0:T(8,128)(2,1)S(1)}, u32[]{:S(2)}, u32[]{:S(2)}) %collective-permute-start.12) | collective-permute-done | bytes 131104 | tf_op jit(solution)/shard_map/ppermute | solution.py:134
  65.4 6.1 %collective-permute-done.13.refs_1_ = bf16[256,256]{1,0:T(8,128)(2,1)S(1)} collective-permute-done((bf16[256,256]{1,0:T(8,128)(2,1)S(1)}, bf16[256,256]{1,0:T(8,128)(2,1)S(1)}, u32[]{:S(2)}, u32[]{:S(2)}) %collective-permute-start.13) | collective-permute-done | bytes 131104 | tf_op jit(solution)/shard_map/ppermute | solution.py:134
  71.5 0.9 %shard_map.106 = bf16[256,256]{1,0:T(8,128)(2,1)} custom-call(f32[256,256]{1,0:T(8,128)S(1)} %get-tuple-element.31.kept, bf16[256,256]{1,0:T(8,128)(2,1)S(1)} %slice_bitcast_fusion.1.from_y, bf16[256,256]{1,0:T(8,128)(2,1)S(1)} %collective-permute-done.12.refs_0_, bf16[256,256]{1,0:T(8,128)(2,1)S(1)} %collective-permute-done.13.refs_1_, ...), custom_call_target="tpu_custom_call" | custom-call | flops 33554432 | bytes 1048576 | tf_op jit(solution)/shard_map/pallas_call | solution.py:28
  72.4 0.6 slice.45
  73.0 0.7 maximum_select_fusion
  (28 shorter events, 0.2 us)
Async XLA Ops:
  0.6 6.8 %copy-start.3 = (bf16[256,256]{1,0:T(8,128)(2,1)S(1)}, bf16[256,256]{1,0:T(8,128)(2,1)}, u32[]{:S(2)}) copy-start(bf16[256,256]{1,0:T(8,128)(2,1)} %refs_0_.1) | copy-start | bytes 393220
  0.6 28.6 %copy-start = (bf16[256,256]{1,0:T(8,128)(2,1)S(1)}, bf16[256,256]{1,0:T(8,128)(2,1)}, u32[]{:S(2)}) copy-start(bf16[256,256]{1,0:T(8,128)(2,1)} %refs_3_.1) | copy-start | bytes 393220
  0.7 28.6 %copy-start.9 = (f32[256]{0:T(256)S(1)}, f32[256]{0:T(256)}, u32[]{:S(2)}) copy-start(f32[256]{0:T(256)} %param.9) | copy-start | bytes 3076
  0.7 28.6 %copy-start.8 = (bf16[256,256]{1,0:T(8,128)(2,1)S(1)}, bf16[256,256]{1,0:T(8,128)(2,1)}, u32[]{:S(2)}) copy-start(bf16[256,256]{1,0:T(8,128)(2,1)} %cotangent.1) | copy-start | bytes 393220
  1.4 0.7 copy-start.10
  5.1 21.8 %collective-permute-start = (bf16[8,256,256]{2,1,0:T(8,128)(2,1)S(1)}, bf16[8,256,256]{2,1,0:T(8,128)(2,1)S(1)}, u32[]{:S(2)}, u32[]{:S(2)}) collective-permute-start(bf16[8,256,256]{2,1,0:T(8,128)(2,1)S(1)} %get-tuple-element.17), channel_id=1, source_target_pairs={{0,1},{1,0},{2,3},{3,2},{4,5},{5,4},{6,7},{7,6},{8,9},{9,8},{10,11... | collective-permute-start | bytes 3145736 | tf_op jit(solution)/shard_map/ppermute | solution.py:134
  7.4 8.0 %collective-permute-start.2 = (bf16[256,256]{1,0:T(8,128)(2,1)S(1)}, bf16[256,256]{1,0:T(8,128)(2,1)S(1)}, u32[]{:S(2)}, u32[]{:S(2)}) collective-permute-start(bf16[256,256]{1,0:T(8,128)(2,1)S(1)} %copy-done.3), channel_id=1, source_target_pairs={{0,4},{1,5},{2,6},{3,7},{4,0},{5,1},{6,2},{7,3},{8,12},{9,13},{10,... | collective-permute-start | bytes 393224 | tf_op jit(solution)/shard_map/ppermute | solution.py:134
  8.8 9.3 %collective-permute-start.4 = (bf16[256,256]{1,0:T(8,128)(2,1)S(1)}, bf16[256,256]{1,0:T(8,128)(2,1)S(1)}, u32[]{:S(2)}, u32[]{:S(2)}) collective-permute-start(bf16[256,256]{1,0:T(8,128)(2,1)S(1)} %copy-done.3), channel_id=1, source_target_pairs={{0,8},{1,9},{2,10},{3,11},{4,12},{5,13},{6,14},{7,15},{8,0},{9,1},... | collective-permute-start | bytes 393224 | tf_op jit(solution)/shard_map/ppermute | solution.py:134
  11.3 10.1 %collective-permute-start.6 = (bf16[256,256]{1,0:T(8,128)(2,1)S(1)}, bf16[256,256]{1,0:T(8,128)(2,1)S(1)}, u32[]{:S(2)}, u32[]{:S(2)}) collective-permute-start(bf16[256,256]{1,0:T(8,128)(2,1)S(1)} %copy-done.3), channel_id=1, source_target_pairs={{0,12},{1,13},{2,14},{3,15},{4,8},{5,9},{6,10},{7,11},{8,4},{9,5},... | collective-permute-start | bytes 393224 | tf_op jit(solution)/shard_map/ppermute | solution.py:134
  12.3 11.3 %collective-permute-start.1 = (bf16[256,256]{1,0:T(8,128)(2,1)S(1)}, bf16[256,256]{1,0:T(8,128)(2,1)S(1)}, u32[]{:S(2)}, u32[]{:S(2)}) collective-permute-start(bf16[256,256]{1,0:T(8,128)(2,1)S(1)} %copy-done.3), channel_id=1, source_target_pairs={{0,2},{1,3},{2,0},{3,1},{4,6},{5,7},{6,4},{7,5},{8,10},{9,11},{10,... | collective-permute-start | bytes 393224 | tf_op jit(solution)/shard_map/ppermute | solution.py:134
  15.4 8.2 %collective-permute-start.3 = (bf16[256,256]{1,0:T(8,128)(2,1)S(1)}, bf16[256,256]{1,0:T(8,128)(2,1)S(1)}, u32[]{:S(2)}, u32[]{:S(2)}) collective-permute-start(bf16[256,256]{1,0:T(8,128)(2,1)S(1)} %collective-permute-done.2.refs_2_), channel_id=1, source_target_pairs={{0,2},{1,3},{2,0},{3,1},{4,6},{5,7},{6,4},{7,5},{8,10},{9,11},{10,... | collective-permute-start | bytes 393224 | tf_op jit(solution)/shard_map/ppermute | solution.py:134
  18.1 5.6 %collective-permute-start.5 = (bf16[256,256]{1,0:T(8,128)(2,1)S(1)}, bf16[256,256]{1,0:T(8,128)(2,1)S(1)}, u32[]{:S(2)}, u32[]{:S(2)}) collective-permute-start(bf16[256,256]{1,0:T(8,128)(2,1)S(1)} %collective-permute-done.4.refs_4_), channel_id=1, source_target_pairs={{0,2},{1,3},{2,0},{3,1},{4,6},{5,7},{6,4},{7,5},{8,10},{9,11},{10,... | collective-permute-start | bytes 393224 | tf_op jit(solution)/shard_map/ppermute | solution.py:134
  21.5 5.4 %collective-permute-start.7 = (bf16[256,256]{1,0:T(8,128)(2,1)S(1)}, bf16[256,256]{1,0:T(8,128)(2,1)S(1)}, u32[]{:S(2)}, u32[]{:S(2)}) collective-permute-start(bf16[256,256]{1,0:T(8,128)(2,1)S(1)} %collective-permute-done.6.refs_6_), channel_id=1, source_target_pairs={{0,2},{1,3},{2,0},{3,1},{4,6},{5,7},{6,4},{7,5},{8,10},{9,11},{10,... | collective-permute-start | bytes 393224 | tf_op jit(solution)/shard_map/ppermute | solution.py:134
  27.6 4.6 %copy-start.1 = (f32[256,256]{1,0:T(8,128)}, f32[256,256]{1,0:T(8,128)S(1)}, u32[]{:S(2)}) copy-start(f32[256,256]{1,0:T(8,128)S(1)} %get-tuple-element.19.partner) | copy-start | bytes 786436
  27.6 1.6 %collective-permute-start.8 = (f32[256,256]{1,0:T(8,128)S(1)}, f32[256,256]{1,0:T(8,128)S(1)}, u32[]{:S(2)}, u32[]{:S(2)}) collective-permute-start(f32[256,256]{1,0:T(8,128)S(1)} %get-tuple-element.19.partner), channel_id=1, source_target_pairs={{0,1},{1,0},{2,3},{3,2},{4,5},{5,4},{6,7},{7,6},{8,9},{9,8},{10,11... | collective-permute-start | bytes 786440 | tf_op jit(solution)/shard_map/ppermute | solution.py:134
  30.2 1.3 %collective-permute-start.9 = (bf16[256,256]{1,0:T(8,128)(2,1)S(1)}, bf16[256,256]{1,0:T(8,128)(2,1)S(1)}, u32[]{:S(2)}, u32[]{:S(2)}) collective-permute-start(bf16[256,256]{1,0:T(8,128)(2,1)S(1)} %get-tuple-element.21.grad), channel_id=1, source_target_pairs={{0,1},{1,0},{2,3},{3,2},{4,5},{5,4},{6,7},{7,6},{8,9},{9,8},{10,11... | collective-permute-start | bytes 393224 | tf_op jit(solution)/shard_map/ppermute | solution.py:134
  30.3 0.7 copy-start.4
  31.5 0.6 copy-start.6
  32.2 1.0 %copy-start.2 = (f32[256,256]{1,0:T(8,128)S(1)}, f32[256,256]{1,0:T(8,128)}, u32[]{:S(2)}) copy-start(f32[256,256]{1,0:T(8,128)} %copy-done.1) | copy-start | bytes 786436
  33.1 0.9 %copy-start.5 = (bf16[256,256]{1,0:T(8,128)(2,1)S(1)}, bf16[256,256]{1,0:T(8,128)(2,1)}, u32[]{:S(2)}) copy-start(bf16[256,256]{1,0:T(8,128)(2,1)} %copy-done.4) | copy-start | bytes 393220
  34.0 0.9 %copy-start.7 = (bf16[256,256]{1,0:T(8,128)(2,1)S(1)}, bf16[256,256]{1,0:T(8,128)(2,1)}, u32[]{:S(2)}) copy-start(bf16[256,256]{1,0:T(8,128)(2,1)} %copy-done.6) | copy-start | bytes 393220
  36.6 1.4 %collective-permute-start.15 = (f32[136,256]{1,0:T(8,128)S(1)}, f32[136,256]{1,0:T(8,128)S(1)}, u32[]{:S(2)}, u32[]{:S(2)}) collective-permute-start(f32[136,256]{1,0:T(8,128)S(1)} %get-tuple-element.27), channel_id=1, source_target_pairs={{0,1},{1,0},{2,3},{3,2},{4,5},{5,4},{6,7},{7,6},{8,9},{9,8},{10,11... | collective-permute-start | bytes 417800 | tf_op jit(solution)/shard_map/ppermute | solution.py:134
  37.9 6.6 %collective-permute-start.16 = (f32[136,256]{1,0:T(8,128)S(1)}, f32[136,256]{1,0:T(8,128)S(1)}, u32[]{:S(2)}, u32[]{:S(2)}) collective-permute-start(f32[136,256]{1,0:T(8,128)S(1)} %add.27), channel_id=1, source_target_pairs={{0,2},{1,3},{2,0},{3,1},{4,6},{5,7},{6,4},{7,5},{8,10},{9,11},{10,... | collective-permute-start | bytes 417800 | tf_op jit(solution)/shard_map/ppermute | solution.py:134
  39.8 14.9 %collective-permute-start.11 = (bf16[2,256,256]{2,1,0:T(8,128)(2,1)}, bf16[2,256,256]{2,1,0:T(8,128)(2,1)S(1)}, u32[]{:S(2)}, u32[]{:S(2)}) collective-permute-start(bf16[2,256,256]{2,1,0:T(8,128)(2,1)} %get-tuple-element.25), channel_id=1, source_target_pairs={{0,2},{1,3},{2,0},{3,1},{4,6},{5,7},{6,4},{7,5},{8,10},{9,11},{10,... | collective-permute-start | bytes 786440 | tf_op jit(solution)/shard_map/ppermute | solution.py:134
  40.0 14.9 %collective-permute-start.10 = (bf16[2,256,256]{2,1,0:T(8,128)(2,1)}, bf16[2,256,256]{2,1,0:T(8,128)(2,1)S(1)}, u32[]{:S(2)}, u32[]{:S(2)}) collective-permute-start(bf16[2,256,256]{2,1,0:T(8,128)(2,1)} %get-tuple-element.24), channel_id=1, source_target_pairs={{0,2},{1,3},{2,0},{3,1},{4,6},{5,7},{6,4},{7,5},{8,10},{9,11},{10,... | collective-permute-start | bytes 786440 | tf_op jit(solution)/shard_map/ppermute | solution.py:134
  44.5 6.0 %collective-permute-start.17 = (f32[136,256]{1,0:T(8,128)S(1)}, f32[136,256]{1,0:T(8,128)S(1)}, u32[]{:S(2)}, u32[]{:S(2)}) collective-permute-start(f32[136,256]{1,0:T(8,128)S(1)} %add.28), channel_id=1, source_target_pairs={{0,4},{1,5},{2,6},{3,7},{4,0},{5,1},{6,2},{7,3},{8,12},{9,13},{10,... | collective-permute-start | bytes 417800 | tf_op jit(solution)/shard_map/ppermute | solution.py:134
  50.6 11.0 %collective-permute-start.18 = (f32[136,256]{1,0:T(8,128)S(1)}, f32[136,256]{1,0:T(8,128)S(1)}, u32[]{:S(2)}, u32[]{:S(2)}) collective-permute-start(f32[136,256]{1,0:T(8,128)S(1)} %add.29), channel_id=1, source_target_pairs={{0,8},{1,9},{2,10},{3,11},{4,12},{5,13},{6,14},{7,15},{8,0},{9,1},... | collective-permute-start | bytes 417800 | tf_op jit(solution)/shard_map/ppermute | solution.py:134
  55.1 10.3 %collective-permute-start.12 = (bf16[256,256]{1,0:T(8,128)(2,1)S(1)}, bf16[256,256]{1,0:T(8,128)(2,1)S(1)}, u32[]{:S(2)}, u32[]{:S(2)}) collective-permute-start(bf16[256,256]{1,0:T(8,128)(2,1)S(1)} %get-tuple-element.29), channel_id=1, source_target_pairs={{0,12},{1,13},{2,14},{3,15},{4,8},{5,9},{6,10},{7,11},{8,4},{9,5},... | collective-permute-start | bytes 393224 | tf_op jit(solution)/shard_map/ppermute | solution.py:134
  60.9 10.5 %collective-permute-start.13 = (bf16[256,256]{1,0:T(8,128)(2,1)S(1)}, bf16[256,256]{1,0:T(8,128)(2,1)S(1)}, u32[]{:S(2)}, u32[]{:S(2)}) collective-permute-start(bf16[256,256]{1,0:T(8,128)(2,1)S(1)} %get-tuple-element.28), channel_id=1, source_target_pairs={{0,8},{1,9},{2,10},{3,11},{4,12},{5,13},{6,14},{7,15},{8,0},{9,1},... | collective-permute-start | bytes 393224 | tf_op jit(solution)/shard_map/ppermute | solution.py:134
  60.9 10.5 %collective-permute-start.14 = (bf16[256,256]{1,0:T(8,128)(2,1)S(1)}, bf16[256,256]{1,0:T(8,128)(2,1)S(1)}, u32[]{:S(2)}, u32[]{:S(2)}) collective-permute-start(bf16[256,256]{1,0:T(8,128)(2,1)S(1)} %get-tuple-element.30), channel_id=1, source_target_pairs={{0,4},{1,5},{2,6},{3,7},{4,0},{5,1},{6,2},{7,3},{8,12},{9,13},{10,... | collective-permute-start | bytes 393224 | tf_op jit(solution)/shard_map/ppermute | solution.py:134
  61.6 11.3 %collective-permute-start.19 = (f32[128,256]{1,0:T(8,128)S(1)}, f32[128,256]{1,0:T(8,128)S(1)}, u32[]{:S(2)}, u32[]{:S(2)}) collective-permute-start(f32[128,256]{1,0:T(8,128)S(1)} %slice.44), channel_id=1, source_target_pairs={{0,1},{1,0},{2,3},{3,2},{4,5},{5,4},{6,7},{7,6},{8,9},{9,8},{10,11... | collective-permute-start | bytes 393224 | tf_op jit(solution)/shard_map/ppermute | solution.py:134

commit v2 on v1

v2 whole, which is shorter than its diff:
```python
import functools

import jax
import jax.numpy as jnp
from jax import lax
from jax.experimental import pallas as pl
from jax.experimental.pallas import tpu as pltpu
from jax.sharding import PartitionSpec as P

F32 = jnp.float32
BF16 = jnp.bfloat16
VMEM = pl.BlockSpec(memory_space=pltpu.VMEM)
SMEM = pl.BlockSpec(memory_space=pltpu.SMEM)
MIB = 1024 * 1024
PIECES = 8
JOIN = 20000000


def dot(a, b):
    return jnp.dot(a, b, preferred_element_type=F32)


def halves(x):
    high = x.astype(BF16)
    return high, (x - high.astype(F32)).astype(BF16)


def at(pieces, index):
    depth = pieces[0].shape[0]
    return pieces[index // depth][index % depth]


def call(kernel, out_shape, args, in_specs=None, scratch=(), flops=0, moved=0, limit=8):
    many = isinstance(out_shape, (list, tuple))
    return pl.pallas_call(
        kernel,
        out_shape=out_shape,
        in_specs=in_specs or [VMEM] * len(args),
        out_specs=[VMEM] * len(out_shape) if many else VMEM,
        scratch_shapes=list(scratch),
        compiler_params=pltpu.CompilerParams(vmem_limit_bytes=limit * MIB),
        cost_estimate=pl.CostEstimate(flops=flops, bytes_accessed=moved, transcendentals=0),
    )(*args)


def merge_kernel(parity, columns, live, me, tiles, *refs):
    others, (held, head, following, sems) = refs[:-4], refs[-4:]
    depth, side = others[0].shape[:2]
    strip = side // 4

    def clear(index, carry):
        head[index] = -1
        return carry

    lax.fori_loop(0, head.shape[0], clear, 0)

    def link(slot, carry):
        where = lax.bitwise_xor(columns[slot], me[0])
        following[slot] = head[where]
        head[where] = slot
        return carry

    lax.fori_loop(0, live[0], link, 0)

    def fetch(slot):
        return pltpu.make_async_copy(tiles.at[slot], held.at[slot], sems.at[slot])

    def chain(index, act):
        def step(slot):
            act(fetch(slot))
            return following[slot]

        lax.while_loop(lambda slot: slot >= 0, step, head[index])

    outs = [(parity + 2 * depth * index, out) for index, out in enumerate(others)]

    def start(base, index, carry):
        chain(2 * index + base, lambda copy: copy.start())
        return carry

    def fill(base, out, index, carry):
        chain(2 * index + base, lambda copy: copy.wait())
        for part in range(4):
            rows = pl.ds(part * strip, strip)

            def add(state, rows=rows):
                slot, total = state
                return following[slot], total + held[slot, rows, :].astype(F32)

            first = (head[2 * index + base], jnp.zeros((strip, side), F32))
            total = lax.while_loop(lambda state: state[0] >= 0, add, first)[1]
            out[index, rows, :] = total.astype(BF16)
        return carry

    for base, out in outs:
        lax.fori_loop(0, out.shape[0], functools.partial(start, base), 0)
    for base, out in outs:
        lax.fori_loop(0, out.shape[0], functools.partial(fill, base, out), 0)


def aggregate_kernel(own, *refs):
    xs, (mine, partner) = refs[PIECES:-2], refs[-2:]
    total_mine = jnp.zeros(mine.shape, F32)
    total_partner = jnp.zeros(mine.shape, F32)
    for index, x in enumerate(xs):
        total_mine += dot(own[index], x[...])
        total_partner += dot(at(refs[:PIECES], index), x[...])
    mine[...] = total_mine
    partner[...] = total_partner


def layer_kernel(mine, received, weight, bias, cotangent, activation, grad_pre_t, grad_bias):
    high, low = halves(mine[...] + received[...])
    pre = dot(high, weight[...]) + dot(low, weight[...]) + bias[...]
    sigma = jax.nn.sigmoid(pre)
    activation[...] = (pre * sigma).astype(BF16)
    grad = (cotangent[...].astype(F32) * sigma * (1.0 + pre * (1.0 - sigma))).astype(BF16)
    grad = grad.astype(F32)
    grad_bias[...] = jnp.broadcast_to(jnp.sum(grad, axis=0, keepdims=True), grad_bias.shape)
    grad_pre_t[...] = grad.T.astype(BF16)


def weight_kernel(core, mine, received, grad, grad_bias, keep, send, whole):
    high, low = halves(mine[...] + received[...])
    whole[...] = (dot(grad[...], high) + dot(grad[...], low)).T
    half = keep.shape[0] - 8
    for out, which in ((keep, core[0]), (send, 1 - core[0])):
        out[pl.ds(0, half), :] = whole[pl.ds(pl.multiple_of(which * half, half), half), :]
        out[pl.ds(half, 8), :] = grad_bias[...]


def backward_kernel(groups, own, grad, grad_other, *refs):
    other, refs = refs[:PIECES], refs[PIECES:]
    sends, keeps = refs[: len(groups)], refs[len(groups) :]
    g, go = grad[...], grad_other[...]
    place = 0
    for send, group in zip(sends, groups):
        for slot, z in enumerate(group):
            near, far = z // 2, z // 2 + 1
            send[slot] = (dot(g, own[far]) + dot(go, at(other, far))).astype(BF16)
            keeps[place][...] = dot(g, own[near]) + dot(go, at(other, near))
            place += 1


def join_kernel(amount, late, *refs):
    refs = refs[late:]
    keeps, received, refs = refs[:amount], refs[amount], refs[amount + 1 :]
    outs = refs[-amount:] if len(refs) == amount else refs[2:-1]
    for slot in range(amount):
        summed = keeps[slot][...] + received[slot].astype(F32)
        outs[slot][...] = summed.astype(outs[slot].dtype)
    if len(refs) > amount:
        refs[-1][...] = refs[0][...] + refs[1][...]


def finish_kernel(core, kept, *refs):
    arrived, refs = refs[:-6], refs[-6:]
    weight, part, part_other, grad_features, grad_weight, grad_bias = refs
    total = kept[...]
    for piece in arrived:
        total += piece[...].astype(F32)
    grad_features[...] = lax.dot_general(
        total.T.astype(BF16), weight[...], (((1,), (1,)), ((), ())), preferred_element_type=F32
    ).astype(BF16)
    half = part_other.shape[0]
    grad_weight[pl.ds(pl.multiple_of(core[0] * half, half), half), :] = part[pl.ds(0, half), :]
    grad_weight[pl.ds(pl.multiple_of((1 - core[0]) * half, half), half), :] = part_other[...]
    grad_bias[...] = part[pl.ds(half, 1), :]


def on_device(features, weight, bias, tiles, tile_col, live_tiles, cotangent):
    side, width = features.shape
    slots = tiles.shape[0]
    count = lax.axis_size("row")
    pairs = count // 2
    me = lax.axis_index("row").astype(jnp.int32)
    core = jnp.bitwise_and(me, 1)

    def swap(x, bit):
        return lax.ppermute(x, "row", [(i, i ^ bit) for i in range(count)])

    block = (side, width)
    wide = jax.ShapeDtypeStruct(block, F32)
    wide_t = jax.ShapeDtypeStruct((width, side), F32)
    zs = list(range(count - 4, -4, -4))
    gathered = {0: features}
    for z in zs[:-1]:
        gathered[z] = swap(features, z)
    gathered[2] = swap(features, 2)
    def merge(parity, pieces):
        return call(
            functools.partial(merge_kernel, parity),
            [jax.ShapeDtypeStruct((pairs // pieces, side, side), BF16)] * pieces,
            (tile_col[0], live_tiles, me[None], tiles),
            in_specs=[SMEM, SMEM, SMEM, pl.BlockSpec(memory_space=pl.ANY)],
            scratch=[
                pltpu.VMEM((slots, side, side), BF16),
                pltpu.SMEM((count,), jnp.int32),
                pltpu.SMEM((slots,), jnp.int32),
                pltpu.SemaphoreType.DMA((slots,)),
            ],
            flops=slots * side * side,
            moved=slots * side * side,
            limit=48,
        )

    (own,) = merge(0, 1)
    sent_other = merge(1, PIECES)
    for z in reversed(zs[:-1]):
        gathered[z + 2] = swap(gathered[z], 2)
    other = [swap(piece, 1) for piece in sent_other]
    xs = [gathered[2 * index] for index in range(pairs)]
    mine, partner = call(
        aggregate_kernel,
        [wide] * 2,
        (own, *other, *xs),
        flops=4 * pairs * side**2 * width,
        moved=3 * pairs * side * width * 2,
    )
    received = swap(partner, 1)
    activation, grad, grad_bias = call(
        layer_kernel,
        [
            jax.ShapeDtypeStruct(block, BF16),
            jax.ShapeDtypeStruct((width, side), BF16),
            jax.ShapeDtypeStruct((8, width), F32),
        ],
        (mine, received, weight, bias[None, :], cotangent),
        flops=4 * side * width**2,
        moved=side * width * 16,
    )
    grad_other = swap(grad, 1)
    half = jax.ShapeDtypeStruct((width // 2 + 8, width), F32)
    part, part_send = call(
        weight_kernel,
        [half] * 2,
        (core[None], mine, received, grad, grad_bias),
        in_specs=[SMEM] + [VMEM] * 4,
        scratch=[pltpu.VMEM((width, width), F32)],
        flops=4 * side * width**2,
        moved=side * width * 12,
    )
    part = part + swap(part_send, 1)
    bits = []
    while 2 << len(bits) < count:
        bits.insert(0, 2 << len(bits))
    share = max(1, len(zs) // 4)
    groups = [zs[:share], zs[share : 2 * share], zs[2 * share :]]
    outs = call(
        functools.partial(backward_kernel, groups),
        [jax.ShapeDtypeStruct((len(group), width, side), BF16) for group in groups]
        + [wide_t] * len(zs),
        (own, grad, grad_other, *other),
        flops=4 * pairs * side**2 * width,
        moved=3 * pairs * side * width * 2,
    )
    sends, keeps = outs[: len(groups)], outs[len(groups) :]
    from_y = [swap(send, 2) for send in sends]
    arrived = []
    place = 0
    for index, group in enumerate(groups):
        shapes = [jax.ShapeDtypeStruct((width, side), BF16 if z else F32) for z in group]
        args = [*keeps[place : place + len(group)], from_y[index]]
        if index != 1:
            shapes.append(half)
            args += [part, swap(part, bits.pop(0))]
        if index == 2:
            args.insert(0, summed[0])
        *summed, = call(
            functools.partial(join_kernel, len(group), index == 2),
            shapes,
            args,
            flops=len(group) * side * width,
            in_specs=[pl.BlockSpec(memory_space=pl.ANY)] * (index == 2) + [VMEM] * (len(args) - (index == 2)),
            moved=JOIN,
        )
        if index != 1:
            part = summed.pop()
        arrived += [swap(piece, z) if z else piece for piece, z in zip(summed, group)]
        place += len(group)
    for bit in bits:
        part = part + swap(part, bit)
    part_other = swap(part[: width // 2], 1)
    grad_features, grad_weight, grad_bias = call(
        finish_kernel,
        [
            jax.ShapeDtypeStruct(block, BF16),
            jax.ShapeDtypeStruct((width, width), F32),
            jax.ShapeDtypeStruct((1, width), F32),
        ],
        (core[None], arrived[-1], *arrived[:-1], weight, part, part_other),
        in_specs=[SMEM] + [VMEM] * (len(zs) + 3),
        flops=2 * side * width**2,
        moved=side * width * 2 * (len(zs) + 4),
    )
    return activation, grad_features, grad_weight, grad_bias[0]


def solution(mesh):
    placed = (
        P(("parts", "row"), None),
        P(),
        P(),
        P(("parts", "row"), None, None),
        P(("parts", "row"), None),
        P(("parts", "row")),
        P(("parts", "row"), None),
    )
    return jax.shard_map(
        on_device,
        mesh=mesh,
        in_specs=placed,
        out_specs=(
            P(("parts", "row"), None),
            P(("parts", "row"), None),
            P("parts", None),
            P("parts"),
        ),
        check_vma=False,
    )
```

time: 73.7 us -> 64.8 us (0.88)
  starting transfers between devices: 31.7 us -> 26.9 us
  local copies, waits for them, and re-layouts: 5.3 us -> 0.68 us
  Pallas kernels: 7.28 us -> 10.5 us
  waiting for transfers between devices: 27 us -> 25 us
  other arithmetic: 0.96 us -> 0.04 us
    ppermute x20 -> x28, starting transfers between devices: 31.7 us -> 26.9 us  [swap(): return lax.ppermute(x, 'row', [(i, i ^ bit) for i in range(count)])]
    unnamed x22 -> x10, local copies, waits for them, and re-layouts: 4.72 us -> 0.67 us
    pallas_call x5 -> x10, Pallas kernels: 7.28 us -> 10.5 us  [call(): pl.pallas_call(kernel, out_shape=out_shape, in_specs=in_specs or [VMEM] *...]
    ppermute x20 -> x28, waiting for transfers between devices: 27 us -> 25 us  [swap(): return lax.ppermute(x, 'row', [(i, i ^ bit) for i in range(count)])]
  transfers between devices with their start and end apart: 20 -> 28, of which waited for: 11 -> 8; matrix products, arithmetic and copies ran while one was open for 1% -> 0% of each run, Pallas kernels for 1% -> 12%
where the time goes in v2:
time: 64.8 us; the launch traced here: 64.6 us
  starting transfers between devices  26.9 us (42%)
  waiting for transfers between devices  25 us (39%)
  Pallas kernels  10.5 us (16%)
  between operations  1.5 us (2%)
  local copies, waits for them, and re-layouts  0.68 us (1%)
    ppermute x28, starting transfers between devices, swap(): return lax.ppermute(x, 'row', [(i, i ^ bit) for i in range(count)])  26.9 us
    ppermute x28, waiting for transfers between devices, swap(): return lax.ppermute(x, 'row', [(i, i ^ bit) for i in range(count)])  25 us
    pallas_call x10, Pallas kernels, call(): pl.pallas_call(kernel, out_shape=out_shape, in_specs=in_specs or [VMEM] *...  10.5 us
  transfers between devices with their start and end apart: 28, of which 8 were waited for; matrix products, arithmetic and copies ran while one was open for 0% of the time, Pallas kernels for 12%

profile of v2, /device:TPU:0, one launch (start us, length us, event | category | flops | bytes accessed | tf_op | source)
XLA Modules:
  0.0 64.6 jit_solution(4932945765970120378)
XLA Ops:
  0.6 4.1 %collective-permute-start.11 = (bf16[256,256]{1,0:T(8,128)(2,1)}, bf16[256,256]{1,0:T(8,128)(2,1)S(1)}, u32[]{:S(2)}, u32[]{:S(2)}) collective-permute-start(bf16[256,256]{1,0:T(8,128)(2,1)} %refs_8_.1), channel_id=1, source_target_pairs={{0,8},{1,9},{2,10},{3,11},{4,12},{5,13},{6,14},{7,15},{8,0},{9,1},... | collective-permute-start | bytes 393224 | tf_op jit(solution)/shard_map/ppermute | solution.py:180
  4.7 1.6 %collective-permute-start.9 = (bf16[256,256]{1,0:T(8,128)(2,1)}, bf16[256,256]{1,0:T(8,128)(2,1)S(1)}, u32[]{:S(2)}, u32[]{:S(2)}) collective-permute-start(bf16[256,256]{1,0:T(8,128)(2,1)} %refs_8_.1), channel_id=1, source_target_pairs={{0,4},{1,5},{2,6},{3,7},{4,0},{5,1},{6,2},{7,3},{8,12},{9,13},{10,... | collective-permute-start | bytes 393224 | tf_op jit(solution)/shard_map/ppermute | solution.py:180
  6.3 1.5 %collective-permute-start.8 = (bf16[256,256]{1,0:T(8,128)(2,1)}, bf16[256,256]{1,0:T(8,128)(2,1)S(1)}, u32[]{:S(2)}, u32[]{:S(2)}) collective-permute-start(bf16[256,256]{1,0:T(8,128)(2,1)} %refs_8_.1), channel_id=1, source_target_pairs={{0,2},{1,3},{2,0},{3,1},{4,6},{5,7},{6,4},{7,5},{8,10},{9,11},{10,... | collective-permute-start | bytes 393224 | tf_op jit(solution)/shard_map/ppermute | solution.py:180
  7.8 0.2 collective-permute-start.13
  8.7 0.6 copy-done.3
  9.4 3.3 %shard_map.103 = (bf16[1,256,256]{2,1,0:T(8,128)(2,1)S(1)}, bf16[1,256,256]{2,1,0:T(8,128)(2,1)S(1)}, bf16[1,256,256]{2,1,0:T(8,128)(2,1)S(1)}, bf16[1,256,256]{...) custom-call(s32[64]{0:T(128)S(1)} %bitcast.5, ...), custom_call_target="tpu_custom_call" | custom-call | flops 4194304 | bytes 4194304 | tf_op jit(solution)/shard_map/pallas_call | solution.py:35
  12.7 0.0 copy-start
  12.7 0.0 copy-start.2
  12.7 0.0 copy-start.4
  12.7 0.1 collective-permute-start
  12.8 0.5 collective-permute-start.1
  13.3 0.1 collective-permute-start.2
  13.4 0.4 collective-permute-start.3
  13.8 1.5 %collective-permute-done.13.refs_14_ = bf16[256,256]{1,0:T(8,128)(2,1)S(1)} collective-permute-done((bf16[256,256]{1,0:T(8,128)(2,1)}, bf16[256,256]{1,0:T(8,128)(2,1)S(1)}, u32[]{:S(2)}, u32[]{:S(2)}) %collective-permute-start.13) | collective-permute-done | bytes 131104 | tf_op jit(solution)/shard_map/ppermute | solution.py:180
  15.3 0.5 collective-permute-start.5
  15.8 0.1 collective-permute-start.6
  15.9 0.4 collective-permute-start.7
  16.3 1.5 %collective-permute-start.12 = (bf16[256,256]{1,0:T(8,128)(2,1)S(1)}, bf16[256,256]{1,0:T(8,128)(2,1)S(1)}, u32[]{:S(2)}, u32[]{:S(2)}) collective-permute-start(bf16[256,256]{1,0:T(8,128)(2,1)S(1)} %collective-permute-done.11.refs_12_), channel_id=1, source_target_pairs={{0,2},{1,3},{2,0},{3,1},{4,6},{5,7},{6,4},{7,5},{8,10},{9,11},{10,... | collective-permute-start | bytes 393224 | tf_op jit(solution)/shard_map/ppermute | solution.py:180
  17.8 0.5 collective-permute-start.10
  18.3 1.5 %collective-permute-start.14 = (bf16[256,256]{1,0:T(8,128)(2,1)S(1)}, bf16[256,256]{1,0:T(8,128)(2,1)S(1)}, u32[]{:S(2)}, u32[]{:S(2)}) collective-permute-start(bf16[256,256]{1,0:T(8,128)(2,1)S(1)} %collective-permute-done.13.refs_14_), channel_id=1, source_target_pairs={{0,2},{1,3},{2,0},{3,1},{4,6},{5,7},{6,4},{7,5},{8,10},{9,11},{10,... | collective-permute-start | bytes 393224 | tf_op jit(solution)/shard_map/ppermute | solution.py:180
  19.9 3.5 %shard_map.102.own = bf16[8,256,256]{2,1,0:T(8,128)(2,1)S(1)} custom-call(s32[64]{0:T(128)S(1)} %bitcast.6, s32[1]{0:T(128)S(6)} %copy.11.live, s32[1]{0:T(128)} %bitcast.1.me, bf16[64,256,256]{2,1,0:T(8,128)(2,1)} %tiles.3), custom_call_target="tpu_custom_call" | custom-call | flops 4194304 | bytes 4194304 | tf_op jit(solution)/shard_map/pallas_call | solution.py:35
  23.4 2.1 %collective-permute-done.10.refs_11_ = bf16[256,256]{1,0:T(8,128)(2,1)S(1)} collective-permute-done((bf16[256,256]{1,0:T(8,128)(2,1)S(1)}, bf16[256,256]{1,0:T(8,128)(2,1)S(1)}, u32[]{:S(2)}, u32[]{:S(2)}) %collective-permute-start.10) | collective-permute-done | bytes 131104 | tf_op jit(solution)/shard_map/ppermute | solution.py:180
  25.5 1.9 %collective-permute-done.14.refs_15_ = bf16[256,256]{1,0:T(8,128)(2,1)S(1)} collective-permute-done((bf16[256,256]{1,0:T(8,128)(2,1)S(1)}, bf16[256,256]{1,0:T(8,128)(2,1)S(1)}, u32[]{:S(2)}, u32[]{:S(2)}) %collective-permute-start.14) | collective-permute-done | bytes 131104 | tf_op jit(solution)/shard_map/ppermute | solution.py:180
  27.4 0.7 %shard_map.104 = (f32[256,256]{1,0:T(8,128)S(1)}, f32[256,256]{1,0:T(8,128)S(1)}) custom-call(bf16[8,256,256]{2,1,0:T(8,128)(2,1)S(1)} %shard_map.102.own, bf16[1,256,256]{2,1,0:T(8,128)(2,1)S(1)} %collective-permute-done.refs_0_, bf16[1,256,256]{2,1,0:T(8,128)(2,1)S(1)} %collective-permute-done.1.refs_1_, ...), custom_call_target="tpu_custom_call" | custom-call | flops 536870912 | bytes 3145728 | tf_op jit(solution)/shard_map/pallas_call | solution.py:35
  28.1 0.1 collective-permute-start.15
  28.2 1.5 %collective-permute-done.15.received = f32[256,256]{1,0:T(8,128)S(1)} collective-permute-done((f32[256,256]{1,0:T(8,128)S(1)}, f32[256,256]{1,0:T(8,128)S(1)}, u32[]{:S(2)}, u32[]{:S(2)}) %collective-permute-start.15) | collective-permute-done | bytes 262176 | tf_op jit(solution)/shard_map/ppermute | solution.py:180
  29.7 1.0 %shard_map.105 = (bf16[256,256]{1,0:T(8,128)(2,1)}, bf16[256,256]{1,0:T(8,128)(2,1)S(1)}, f32[8,256]{1,0:T(8,128)S(1)}) custom-call(f32[256,256]{1,0:T(8,128)S(1)} %get-tuple-element.42.mine, f32[256,256]{1,0:T(8,128)S(1)} %collective-permute-done.15.received, bf16[256,256]{1,0:T(8,128)(2,1)S(1)} %copy-done, f32[1,256]{1,0:T(1,128)S(1)} %bitcast.7, ...), custom_call_target="tpu_custom_call" | custom-call | flops 67108864 | bytes 1048576 | tf_op jit(solution)/shard_map/pallas_call | solution.py:35
  30.7 0.3 shard_map.108
  31.0 0.2 collective-permute-start.20
  31.2 0.4 collective-permute-start.16
  31.6 0.8 %collective-permute-done.20 = f32[136,256]{1,0:T(8,128)S(1)} collective-permute-done((f32[136,256]{1,0:T(8,128)S(1)}, f32[136,256]{1,0:T(8,128)S(1)}, u32[]{:S(2)}, u32[]{:S(2)}) %collective-permute-start.20) | collective-permute-done | bytes 139296 | tf_op jit(solution)/shard_map/ppermute | solution.py:180
  32.4 4.3 %collective-permute-start.21 = (f32[136,256]{1,0:T(8,128)S(1)}, f32[136,256]{1,0:T(8,128)S(1)}, u32[]{:S(2)}, u32[]{:S(2)}) collective-permute-start(f32[136,256]{1,0:T(8,128)S(1)} %add.6.refs_2_), channel_id=1, source_target_pairs={{0,8},{1,9},{2,10},{3,11},{4,12},{5,13},{6,14},{7,15},{8,0},{9,1},... | collective-permute-start | bytes 417800 | tf_op jit(solution)/shard_map/ppermute | solution.py:180
  36.7 0.7 %shard_map.106 = (bf16[1,256,256]{2,1,0:T(8,128)(2,1)S(1)}, bf16[1,256,256]{2,1,0:T(8,128)(2,1)S(1)}, bf16[2,256,256]{2,1,0:T(8,128)(2,1)S(1)}, f32[256,256]{1,0...) custom-call(bf16[8,256,256]{2,1,0:T(8,128)(2,1)S(1)} %shard_map.102.own, ...), custom_call_target="tpu_custom_call" | custom-call | flops 536870912 | bytes 3145728 | tf_op jit(solution)/shard_map/pallas_call | solution.py:35
  37.5 1.6 %collective-permute-start.19 = (bf16[1,256,256]{2,1,0:T(8,128)(2,1)S(1)}, bf16[1,256,256]{2,1,0:T(8,128)(2,1)S(1)}, u32[]{:S(2)}, u32[]{:S(2)}) collective-permute-start(bf16[1,256,256]{2,1,0:T(8,128)(2,1)S(1)} %get-tuple-element.52), channel_id=1, source_target_pairs={{0,2},{1,3},{2,0},{3,1},{4,6},{5,7},{6,4},{7,5},{8,10},{9,11},{10,... | collective-permute-start | bytes 393224 | tf_op jit(solution)/shard_map/ppermute | solution.py:180
  39.1 0.5 collective-permute-start.18
  39.6 4.4 %collective-permute-done.19.refs_1_ = bf16[1,256,256]{2,1,0:T(8,128)(2,1)S(1)} collective-permute-done((bf16[1,256,256]{2,1,0:T(8,128)(2,1)S(1)}, bf16[1,256,256]{2,1,0:T(8,128)(2,1)S(1)}, u32[]{:S(2)}, u32[]{:S(2)}) %collective-permute-start.19) | collective-permute-done | bytes 131104 | tf_op jit(solution)/shard_map/ppermute | solution.py:180
  44.0 0.1 collective-permute-start.22
  44.1 1.6 %collective-permute-start.17 = (bf16[1,256,256]{2,1,0:T(8,128)(2,1)S(1)}, bf16[1,256,256]{2,1,0:T(8,128)(2,1)S(1)}, u32[]{:S(2)}, u32[]{:S(2)}) collective-permute-start(bf16[1,256,256]{2,1,0:T(8,128)(2,1)S(1)} %get-tuple-element.47), channel_id=1, source_target_pairs={{0,2},{1,3},{2,0},{3,1},{4,6},{5,7},{6,4},{7,5},{8,10},{9,11},{10,... | collective-permute-start | bytes 393224 | tf_op jit(solution)/shard_map/ppermute | solution.py:180
  45.6 5.6 %collective-permute-done.17.refs_1_ = bf16[1,256,256]{2,1,0:T(8,128)(2,1)S(1)} collective-permute-done((bf16[1,256,256]{2,1,0:T(8,128)(2,1)S(1)}, bf16[1,256,256]{2,1,0:T(8,128)(2,1)S(1)}, u32[]{:S(2)}, u32[]{:S(2)}) %collective-permute-start.17) | collective-permute-done | bytes 131104 | tf_op jit(solution)/shard_map/ppermute | solution.py:180
  51.3 0.1 shard_map.110
  51.4 1.6 %collective-permute-start.26 = (f32[136,256]{1,0:T(8,128)S(1)}, f32[136,256]{1,0:T(8,128)S(1)}, u32[]{:S(2)}, u32[]{:S(2)}) collective-permute-start(f32[136,256]{1,0:T(8,128)S(1)} %get-tuple-element.60), channel_id=1, source_target_pairs={{0,2},{1,3},{2,0},{3,1},{4,6},{5,7},{6,4},{7,5},{8,10},{9,11},{10,... | collective-permute-start | bytes 417800 | tf_op jit(solution)/shard_map/ppermute | solution.py:180
  52.9 0.5 collective-permute-start.24
  53.5 1.6 %collective-permute-start.23 = (bf16[256,256]{1,0:T(8,128)(2,1)S(1)}, bf16[256,256]{1,0:T(8,128)(2,1)S(1)}, u32[]{:S(2)}, u32[]{:S(2)}) collective-permute-start(bf16[256,256]{1,0:T(8,128)(2,1)S(1)} %get-tuple-element.58), channel_id=1, source_target_pairs={{0,12},{1,13},{2,14},{3,15},{4,8},{5,9},{6,10},{7,11},{8,4},{9,5},... | collective-permute-start | bytes 393224 | tf_op jit(solution)/shard_map/ppermute | solution.py:180
  55.1 1.3 %collective-permute-start.25 = (bf16[256,256]{1,0:T(8,128)(2,1)S(1)}, bf16[256,256]{1,0:T(8,128)(2,1)S(1)}, u32[]{:S(2)}, u32[]{:S(2)}) collective-permute-start(bf16[256,256]{1,0:T(8,128)(2,1)S(1)} %get-tuple-element.59), channel_id=1, source_target_pairs={{0,4},{1,5},{2,6},{3,7},{4,0},{5,1},{6,2},{7,3},{8,12},{9,13},{10,... | collective-permute-start | bytes 393224 | tf_op jit(solution)/shard_map/ppermute | solution.py:180
  56.4 0.0 collective-permute-done.26
  56.5 0.1 collective-permute-start.27
  56.6 7.1 %collective-permute-done.24.refs_1_ = bf16[256,256]{1,0:T(8,128)(2,1)S(1)} collective-permute-done((bf16[256,256]{1,0:T(8,128)(2,1)S(1)}, bf16[256,256]{1,0:T(8,128)(2,1)S(1)}, u32[]{:S(2)}, u32[]{:S(2)}) %collective-permute-start.24) | collective-permute-done | bytes 131104 | tf_op jit(solution)/shard_map/ppermute | solution.py:180
  63.7 0.9 %shard_map.111 = (bf16[256,256]{1,0:T(8,128)(2,1)}, f32[256,256]{1,0:T(8,128)}, f32[1,256]{1,0:T(1,128)}) custom-call(s32[1]{0:T(128)} %bitcast.3.core, f32[256,256]{1,0:T(8,128)S(1)} %get-tuple-element.57.kept, bf16[256,256]{1,0:T(8,128)(2,1)S(1)} %collective-permute-done.23.refs_0_, bf16[256,256]{1,0:T(8,128)(2,1)S(1)} %collective-permute-done.24.refs_1_, ...), custom_call_target="tpu_custom_call" | custom-call | flops 33554432 | bytes 1048576 | tf_op jit(solution)/shard_map/pallas_call | solution.py:35
  (31 shorter events, 0.2 us)
Async XLA Ops:
  0.6 12.1 %collective-permute-start.11 = (bf16[256,256]{1,0:T(8,128)(2,1)}, bf16[256,256]{1,0:T(8,128)(2,1)S(1)}, u32[]{:S(2)}, u32[]{:S(2)}) collective-permute-start(bf16[256,256]{1,0:T(8,128)(2,1)} %refs_8_.1), channel_id=1, source_target_pairs={{0,8},{1,9},{2,10},{3,11},{4,12},{5,13},{6,14},{7,15},{8,0},{9,1},... | collective-permute-start | bytes 393224 | tf_op jit(solution)/shard_map/ppermute | solution.py:180
  4.7 8.5 %collective-permute-start.9 = (bf16[256,256]{1,0:T(8,128)(2,1)}, bf16[256,256]{1,0:T(8,128)(2,1)S(1)}, u32[]{:S(2)}, u32[]{:S(2)}) collective-permute-start(bf16[256,256]{1,0:T(8,128)(2,1)} %refs_8_.1), channel_id=1, source_target_pairs={{0,4},{1,5},{2,6},{3,7},{4,0},{5,1},{6,2},{7,3},{8,12},{9,13},{10,... | collective-permute-start | bytes 393224 | tf_op jit(solution)/shard_map/ppermute | solution.py:180
  6.3 7.1 %collective-permute-start.8 = (bf16[256,256]{1,0:T(8,128)(2,1)}, bf16[256,256]{1,0:T(8,128)(2,1)S(1)}, u32[]{:S(2)}, u32[]{:S(2)}) collective-permute-start(bf16[256,256]{1,0:T(8,128)(2,1)} %refs_8_.1), channel_id=1, source_target_pairs={{0,2},{1,3},{2,0},{3,1},{4,6},{5,7},{6,4},{7,5},{8,10},{9,11},{10,... | collective-permute-start | bytes 393224 | tf_op jit(solution)/shard_map/ppermute | solution.py:180
  7.8 7.4 %collective-permute-start.13 = (bf16[256,256]{1,0:T(8,128)(2,1)}, bf16[256,256]{1,0:T(8,128)(2,1)S(1)}, u32[]{:S(2)}, u32[]{:S(2)}) collective-permute-start(bf16[256,256]{1,0:T(8,128)(2,1)} %refs_8_.1), channel_id=1, source_target_pairs={{0,12},{1,13},{2,14},{3,15},{4,8},{5,9},{6,10},{7,11},{8,4},{9,5},... | collective-permute-start | bytes 393224 | tf_op jit(solution)/shard_map/ppermute | solution.py:180
  8.7 0.7 %copy-start.3 = (s32[1,64]{1,0:T(1,128)S(1)}, s32[1,64]{1,0:T(1,128)}, u32[]{:S(2)}) copy-start(s32[1,64]{1,0:T(1,128)} %param.11) | copy-start | bytes 772
  9.4 18.0 %copy-start.1 = (bf16[256,256]{1,0:T(8,128)(2,1)S(1)}, bf16[256,256]{1,0:T(8,128)(2,1)}, u32[]{:S(2)}) copy-start(bf16[256,256]{1,0:T(8,128)(2,1)} %refs_8_.1) | copy-start | bytes 393220
  12.7 17.1 %copy-start = (bf16[256,256]{1,0:T(8,128)(2,1)S(1)}, bf16[256,256]{1,0:T(8,128)(2,1)}, u32[]{:S(2)}) copy-start(bf16[256,256]{1,0:T(8,128)(2,1)} %refs_3_.1) | copy-start | bytes 393220
  12.7 17.0 %copy-start.2 = (bf16[256,256]{1,0:T(8,128)(2,1)S(1)}, bf16[256,256]{1,0:T(8,128)(2,1)}, u32[]{:S(2)}) copy-start(bf16[256,256]{1,0:T(8,128)(2,1)} %cotangent.1) | copy-start | bytes 393220
  12.7 17.0 %copy-start.4 = (f32[256]{0:T(256)S(1)}, f32[256]{0:T(256)}, u32[]{:S(2)}) copy-start(f32[256]{0:T(256)} %param.9) | copy-start | bytes 3076
  12.7 2.6 %collective-permute-start = (bf16[1,256,256]{2,1,0:T(8,128)(2,1)S(1)}, bf16[1,256,256]{2,1,0:T(8,128)(2,1)S(1)}, u32[]{:S(2)}, u32[]{:S(2)}) collective-permute-start(bf16[1,256,256]{2,1,0:T(8,128)(2,1)S(1)} %get-tuple-element.34), channel_id=1, source_target_pairs={{0,1},{1,0},{2,3},{3,2},{4,5},{5,4},{6,7},{7,6},{8,9},{9,8},{10,11... | collective-permute-start | bytes 393224 | tf_op jit(solution)/shard_map/ppermute | solution.py:180
  12.8 3.0 %collective-permute-start.1 = (bf16[1,256,256]{2,1,0:T(8,128)(2,1)S(1)}, bf16[1,256,256]{2,1,0:T(8,128)(2,1)S(1)}, u32[]{:S(2)}, u32[]{:S(2)}) collective-permute-start(bf16[1,256,256]{2,1,0:T(8,128)(2,1)S(1)} %get-tuple-element.35), channel_id=1, source_target_pairs={{0,1},{1,0},{2,3},{3,2},{4,5},{5,4},{6,7},{7,6},{8,9},{9,8},{10,11... | collective-permute-start | bytes 393224 | tf_op jit(solution)/shard_map/ppermute | solution.py:180
  13.3 2.6 %collective-permute-start.2 = (bf16[1,256,256]{2,1,0:T(8,128)(2,1)S(1)}, bf16[1,256,256]{2,1,0:T(8,128)(2,1)S(1)}, u32[]{:S(2)}, u32[]{:S(2)}) collective-permute-start(bf16[1,256,256]{2,1,0:T(8,128)(2,1)S(1)} %get-tuple-element.36), channel_id=1, source_target_pairs={{0,1},{1,0},{2,3},{3,2},{4,5},{5,4},{6,7},{7,6},{8,9},{9,8},{10,11... | collective-permute-start | bytes 393224 | tf_op jit(solution)/shard_map/ppermute | solution.py:180
  13.4 2.9 %collective-permute-start.3 = (bf16[1,256,256]{2,1,0:T(8,128)(2,1)S(1)}, bf16[1,256,256]{2,1,0:T(8,128)(2,1)S(1)}, u32[]{:S(2)}, u32[]{:S(2)}) collective-permute-start(bf16[1,256,256]{2,1,0:T(8,128)(2,1)S(1)} %get-tuple-element.37), channel_id=1, source_target_pairs={{0,1},{1,0},{2,3},{3,2},{4,5},{5,4},{6,7},{7,6},{8,9},{9,8},{10,11... | collective-permute-start | bytes 393224 | tf_op jit(solution)/shard_map/ppermute | solution.py:180
  15.3 2.6 %collective-permute-start.4 = (bf16[1,256,256]{2,1,0:T(8,128)(2,1)S(1)}, bf16[1,256,256]{2,1,0:T(8,128)(2,1)S(1)}, u32[]{:S(2)}, u32[]{:S(2)}) collective-permute-start(bf16[1,256,256]{2,1,0:T(8,128)(2,1)S(1)} %get-tuple-element.38), channel_id=1, source_target_pairs={{0,1},{1,0},{2,3},{3,2},{4,5},{5,4},{6,7},{7,6},{8,9},{9,8},{10,11... | collective-permute-start | bytes 393224 | tf_op jit(solution)/shard_map/ppermute | solution.py:180
  15.3 3.1 %collective-permute-start.5 = (bf16[1,256,256]{2,1,0:T(8,128)(2,1)S(1)}, bf16[1,256,256]{2,1,0:T(8,128)(2,1)S(1)}, u32[]{:S(2)}, u32[]{:S(2)}) collective-permute-start(bf16[1,256,256]{2,1,0:T(8,128)(2,1)S(1)} %get-tuple-element.39), channel_id=1, source_target_pairs={{0,1},{1,0},{2,3},{3,2},{4,5},{5,4},{6,7},{7,6},{8,9},{9,8},{10,11... | collective-permute-start | bytes 393224 | tf_op jit(solution)/shard_map/ppermute | solution.py:180
  15.8 7.6 %collective-permute-start.6 = (bf16[1,256,256]{2,1,0:T(8,128)(2,1)S(1)}, bf16[1,256,256]{2,1,0:T(8,128)(2,1)S(1)}, u32[]{:S(2)}, u32[]{:S(2)}) collective-permute-start(bf16[1,256,256]{2,1,0:T(8,128)(2,1)S(1)} %get-tuple-element.40), channel_id=1, source_target_pairs={{0,1},{1,0},{2,3},{3,2},{4,5},{5,4},{6,7},{7,6},{8,9},{9,8},{10,11... | collective-permute-start | bytes 393224 | tf_op jit(solution)/shard_map/ppermute | solution.py:180
  15.9 7.5 %collective-permute-start.7 = (bf16[1,256,256]{2,1,0:T(8,128)(2,1)S(1)}, bf16[1,256,256]{2,1,0:T(8,128)(2,1)S(1)}, u32[]{:S(2)}, u32[]{:S(2)}) collective-permute-start(bf16[1,256,256]{2,1,0:T(8,128)(2,1)S(1)} %get-tuple-element.41), channel_id=1, source_target_pairs={{0,1},{1,0},{2,3},{3,2},{4,5},{5,4},{6,7},{7,6},{8,9},{9,8},{10,11... | collective-permute-start | bytes 393224 | tf_op jit(solution)/shard_map/ppermute | solution.py:180
  16.3 7.1 %collective-permute-start.12 = (bf16[256,256]{1,0:T(8,128)(2,1)S(1)}, bf16[256,256]{1,0:T(8,128)(2,1)S(1)}, u32[]{:S(2)}, u32[]{:S(2)}) collective-permute-start(bf16[256,256]{1,0:T(8,128)(2,1)S(1)} %collective-permute-done.11.refs_12_), channel_id=1, source_target_pairs={{0,2},{1,3},{2,0},{3,1},{4,6},{5,7},{6,4},{7,5},{8,10},{9,11},{10,... | collective-permute-start | bytes 393224 | tf_op jit(solution)/shard_map/ppermute | solution.py:180
  17.8 7.6 %collective-permute-start.10 = (bf16[256,256]{1,0:T(8,128)(2,1)S(1)}, bf16[256,256]{1,0:T(8,128)(2,1)S(1)}, u32[]{:S(2)}, u32[]{:S(2)}) collective-permute-start(bf16[256,256]{1,0:T(8,128)(2,1)S(1)} %collective-permute-done.9.refs_10_), channel_id=1, source_target_pairs={{0,2},{1,3},{2,0},{3,1},{4,6},{5,7},{6,4},{7,5},{8,10},{9,11},{10,... | collective-permute-start | bytes 393224 | tf_op jit(solution)/shard_map/ppermute | solution.py:180
  18.3 9.1 %collective-permute-start.14 = (bf16[256,256]{1,0:T(8,128)(2,1)S(1)}, bf16[256,256]{1,0:T(8,128)(2,1)S(1)}, u32[]{:S(2)}, u32[]{:S(2)}) collective-permute-start(bf16[256,256]{1,0:T(8,128)(2,1)S(1)} %collective-permute-done.13.refs_14_), channel_id=1, source_target_pairs={{0,2},{1,3},{2,0},{3,1},{4,6},{5,7},{6,4},{7,5},{8,10},{9,11},{10,... | collective-permute-start | bytes 393224 | tf_op jit(solution)/shard_map/ppermute | solution.py:180
  28.1 1.6 %collective-permute-start.15 = (f32[256,256]{1,0:T(8,128)S(1)}, f32[256,256]{1,0:T(8,128)S(1)}, u32[]{:S(2)}, u32[]{:S(2)}) collective-permute-start(f32[256,256]{1,0:T(8,128)S(1)} %get-tuple-element.43), channel_id=1, source_target_pairs={{0,1},{1,0},{2,3},{3,2},{4,5},{5,4},{6,7},{7,6},{8,9},{9,8},{10,11... | collective-permute-start | bytes 786440 | tf_op jit(solution)/shard_map/ppermute | solution.py:180
  31.0 1.4 %collective-permute-start.20 = (f32[136,256]{1,0:T(8,128)S(1)}, f32[136,256]{1,0:T(8,128)S(1)}, u32[]{:S(2)}, u32[]{:S(2)}) collective-permute-start(f32[136,256]{1,0:T(8,128)S(1)} %get-tuple-element.55), channel_id=1, source_target_pairs={{0,1},{1,0},{2,3},{3,2},{4,5},{5,4},{6,7},{7,6},{8,9},{9,8},{10,11... | collective-permute-start | bytes 417800 | tf_op jit(solution)/shard_map/ppermute | solution.py:180
  31.2 5.6 %collective-permute-start.16 = (bf16[256,256]{1,0:T(8,128)(2,1)S(1)}, bf16[256,256]{1,0:T(8,128)(2,1)S(1)}, u32[]{:S(2)}, u32[]{:S(2)}) collective-permute-start(bf16[256,256]{1,0:T(8,128)(2,1)S(1)} %get-tuple-element.45.grad), channel_id=1, source_target_pairs={{0,1},{1,0},{2,3},{3,2},{4,5},{5,4},{6,7},{7,6},{8,9},{9,8},{10,11... | collective-permute-start | bytes 393224 | tf_op jit(solution)/shard_map/ppermute | solution.py:180
  32.4 11.5 %collective-permute-start.21 = (f32[136,256]{1,0:T(8,128)S(1)}, f32[136,256]{1,0:T(8,128)S(1)}, u32[]{:S(2)}, u32[]{:S(2)}) collective-permute-start(f32[136,256]{1,0:T(8,128)S(1)} %add.6.refs_2_), channel_id=1, source_target_pairs={{0,8},{1,9},{2,10},{3,11},{4,12},{5,13},{6,14},{7,15},{8,0},{9,1},... | collective-permute-start | bytes 417800 | tf_op jit(solution)/shard_map/ppermute | solution.py:180
  37.5 6.4 %collective-permute-start.19 = (bf16[1,256,256]{2,1,0:T(8,128)(2,1)S(1)}, bf16[1,256,256]{2,1,0:T(8,128)(2,1)S(1)}, u32[]{:S(2)}, u32[]{:S(2)}) collective-permute-start(bf16[1,256,256]{2,1,0:T(8,128)(2,1)S(1)} %get-tuple-element.52), channel_id=1, source_target_pairs={{0,2},{1,3},{2,0},{3,1},{4,6},{5,7},{6,4},{7,5},{8,10},{9,11},{10,... | collective-permute-start | bytes 393224 | tf_op jit(solution)/shard_map/ppermute | solution.py:180
  39.1 12.2 %collective-permute-start.18 = (bf16[2,256,256]{2,1,0:T(8,128)(2,1)S(1)}, bf16[2,256,256]{2,1,0:T(8,128)(2,1)S(1)}, u32[]{:S(2)}, u32[]{:S(2)}) collective-permute-start(bf16[2,256,256]{2,1,0:T(8,128)(2,1)S(1)} %get-tuple-element.50), channel_id=1, source_target_pairs={{0,2},{1,3},{2,0},{3,1},{4,6},{5,7},{6,4},{7,5},{8,10},{9,11},{10,... | collective-permute-start | bytes 786440 | tf_op jit(solution)/shard_map/ppermute | solution.py:180
  44.0 7.3 %collective-permute-start.22 = (f32[136,256]{1,0:T(8,128)S(1)}, f32[136,256]{1,0:T(8,128)S(1)}, u32[]{:S(2)}, u32[]{:S(2)}) collective-permute-start(f32[136,256]{1,0:T(8,128)S(1)} %get-tuple-element.56.refs_4_), channel_id=1, source_target_pairs={{0,4},{1,5},{2,6},{3,7},{4,0},{5,1},{6,2},{7,3},{8,12},{9,13},{10,... | collective-permute-start | bytes 417800 | tf_op jit(solution)/shard_map/ppermute | solution.py:180
  44.1 7.2 %collective-permute-start.17 = (bf16[1,256,256]{2,1,0:T(8,128)(2,1)S(1)}, bf16[1,256,256]{2,1,0:T(8,128)(2,1)S(1)}, u32[]{:S(2)}, u32[]{:S(2)}) collective-permute-start(bf16[1,256,256]{2,1,0:T(8,128)(2,1)S(1)} %get-tuple-element.47), channel_id=1, source_target_pairs={{0,2},{1,3},{2,0},{3,1},{4,6},{5,7},{6,4},{7,5},{8,10},{9,11},{10,... | collective-permute-start | bytes 393224 | tf_op jit(solution)/shard_map/ppermute | solution.py:180
  51.4 5.1 %collective-permute-start.26 = (f32[136,256]{1,0:T(8,128)S(1)}, f32[136,256]{1,0:T(8,128)S(1)}, u32[]{:S(2)}, u32[]{:S(2)}) collective-permute-start(f32[136,256]{1,0:T(8,128)S(1)} %get-tuple-element.60), channel_id=1, source_target_pairs={{0,2},{1,3},{2,0},{3,1},{4,6},{5,7},{6,4},{7,5},{8,10},{9,11},{10,... | collective-permute-start | bytes 417800 | tf_op jit(solution)/shard_map/ppermute | solution.py:180
  52.9 10.8 %collective-permute-start.24 = (bf16[256,256]{1,0:T(8,128)(2,1)S(1)}, bf16[256,256]{1,0:T(8,128)(2,1)S(1)}, u32[]{:S(2)}, u32[]{:S(2)}) collective-permute-start(bf16[256,256]{1,0:T(8,128)(2,1)S(1)} %shard_map.107.refs_0_), channel_id=1, source_target_pairs={{0,8},{1,9},{2,10},{3,11},{4,12},{5,13},{6,14},{7,15},{8,0},{9,1},... | collective-permute-start | bytes 393224 | tf_op jit(solution)/shard_map/ppermute | solution.py:180
  53.5 10.2 %collective-permute-start.23 = (bf16[256,256]{1,0:T(8,128)(2,1)S(1)}, bf16[256,256]{1,0:T(8,128)(2,1)S(1)}, u32[]{:S(2)}, u32[]{:S(2)}) collective-permute-start(bf16[256,256]{1,0:T(8,128)(2,1)S(1)} %get-tuple-element.58), channel_id=1, source_target_pairs={{0,12},{1,13},{2,14},{3,15},{4,8},{5,9},{6,10},{7,11},{8,4},{9,5},... | collective-permute-start | bytes 393224 | tf_op jit(solution)/shard_map/ppermute | solution.py:180
  55.1 8.6 %collective-permute-start.25 = (bf16[256,256]{1,0:T(8,128)(2,1)S(1)}, bf16[256,256]{1,0:T(8,128)(2,1)S(1)}, u32[]{:S(2)}, u32[]{:S(2)}) collective-permute-start(bf16[256,256]{1,0:T(8,128)(2,1)S(1)} %get-tuple-element.59), channel_id=1, source_target_pairs={{0,4},{1,5},{2,6},{3,7},{4,0},{5,1},{6,2},{7,3},{8,12},{9,13},{10,... | collective-permute-start | bytes 393224 | tf_op jit(solution)/shard_map/ppermute | solution.py:180
  56.5 7.2 %collective-permute-start.27 = (f32[128,256]{1,0:T(8,128)S(1)}, f32[128,256]{1,0:T(8,128)S(1)}, u32[]{:S(2)}, u32[]{:S(2)}) collective-permute-start(f32[128,256]{1,0:T(8,128)S(1)} %slice.4), channel_id=1, source_target_pairs={{0,1},{1,0},{2,3},{3,2},{4,5},{5,4},{6,7},{7,6},{8,9},{9,8},{10,11... | collective-permute-start | bytes 393224 | tf_op jit(solution)/shard_map/ppermute | solution.py:180

commit v3 on v2

--- a/solution.py
+++ b/solution.py
@@ -13,7 +13,6 @@
 SMEM = pl.BlockSpec(memory_space=pltpu.SMEM)
 MIB = 1024 * 1024
 PIECES = 8
-JOIN = 20000000
 
 
 def dot(a, b):
@@ -123,10 +122,11 @@
 def weight_kernel(core, mine, received, grad, grad_bias, keep, send, whole):
     high, low = halves(mine[...] + received[...])
     whole[...] = (dot(grad[...], high) + dot(grad[...], low)).T
-    half = keep.shape[0] - 8
+    half = keep.shape[0] - 16
     for out, which in ((keep, core[0]), (send, 1 - core[0])):
         out[pl.ds(0, half), :] = whole[pl.ds(pl.multiple_of(which * half, half), half), :]
         out[pl.ds(half, 8), :] = grad_bias[...]
+        out[pl.ds(half + 8, 8), :] = jnp.zeros_like(grad_bias)
 
 
 def backward_kernel(groups, own, grad, grad_other, *refs):
@@ -142,15 +142,26 @@
             place += 1
 
 
-def join_kernel(amount, late, *refs):
-    refs = refs[late:]
-    keeps, received, refs = refs[:amount], refs[amount], refs[amount + 1 :]
-    outs = refs[-amount:] if len(refs) == amount else refs[2:-1]
-    for slot in range(amount):
-        summed = keeps[slot][...] + received[slot].astype(F32)
+def join_kernel(keeps_amount, *refs):
+    received, outs = refs[keeps_amount], refs[keeps_amount + 1 :]
+    for slot in range(keeps_amount):
+        summed = refs[slot][...] + received[slot].astype(F32)
         outs[slot][...] = summed.astype(outs[slot].dtype)
-    if len(refs) > amount:
-        refs[-1][...] = refs[0][...] + refs[1][...]
+
+
+def parts_kernel(amount, *refs):
+    out = refs[-1]
+    half = out.shape[0] - 16
+    values = [ref[...].astype(F32) for ref in refs[:amount]]
+    while len(values) > 1:
+        values = [values[i] + values[i + 1] for i in range(0, len(values), 2)]
+    (total,) = values
+    bias = total[half : half + 8] + total[half + 8 :]
+    high, low = halves(bias)
+    out[pl.ds(0, half), :] = total[:half].astype(out.dtype)
+    if out.dtype == F32:
+        high, low = bias, jnp.zeros_like(bias)
+    out[pl.ds(half, 16), :] = jnp.concatenate([high.astype(F32), low.astype(F32)]).astype(out.dtype)
 
 
 def finish_kernel(core, kept, *refs):
@@ -184,9 +195,8 @@
     wide_t = jax.ShapeDtypeStruct((width, side), F32)
     zs = list(range(count - 4, -4, -4))
     gathered = {0: features}
-    for z in zs[:-1]:
+    for z in zs[:-1] + [2]:
         gathered[z] = swap(features, z)
-    gathered[2] = swap(features, 2)
     def merge(parity, pieces):
         return call(
             functools.partial(merge_kernel, parity),
@@ -206,8 +216,8 @@
 
     (own,) = merge(0, 1)
     sent_other = merge(1, PIECES)
-    for z in reversed(zs[:-1]):
-        gathered[z + 2] = swap(gathered[z], 2)
+    for z in zs[:-1]:
+        gathered[z + 2] = swap(gathered[2], z) if z == 4 else swap(gathered[z], 2)
     other = [swap(piece, 1) for piece in sent_other]
     xs = [gathered[2 * index] for index in range(pairs)]
     mine, partner = call(
@@ -230,7 +240,7 @@
         moved=side * width * 16,
     )
     grad_other = swap(grad, 1)
-    half = jax.ShapeDtypeStruct((width // 2 + 8, width), F32)
+    half = jax.ShapeDtypeStruct((width // 2 + 16, width), F32)
     part, part_send = call(
         weight_kernel,
         [half] * 2,
@@ -240,12 +250,19 @@
         flops=4 * side * width**2,
         moved=side * width * 12,
     )
-    part = part + swap(part_send, 1)
-    bits = []
-    while 2 << len(bits) < count:
-        bits.insert(0, 2 << len(bits))
+
+    def add_parts(pieces, dtype, later=()):
+        return call(
+            functools.partial(parts_kernel, len(pieces)),
+            jax.ShapeDtypeStruct(half.shape, dtype),
+            (*pieces, *later),
+            in_specs=[VMEM] * len(pieces) + [pl.BlockSpec(memory_space=pl.ANY)] * len(later),
+            flops=len(pieces) * width**2,
+            moved=len(pieces) * width**2,
+        )
+
     share = max(1, len(zs) // 4)
-    groups = [zs[:share], zs[share : 2 * share], zs[2 * share :]]
+    groups = [zs[start : start + share] for start in range(0, len(zs), share)]
     outs = call(
         functools.partial(backward_kernel, groups),
         [jax.ShapeDtypeStruct((len(group), width, side), BF16) for group in groups]
@@ -256,30 +273,21 @@
     )
     sends, keeps = outs[: len(groups)], outs[len(groups) :]
     from_y = [swap(send, 2) for send in sends]
+    packed = add_parts((part, swap(part_send, 1)), BF16, outs[:1])
+    packed = add_parts([swap(packed, z) if z else packed for z in reversed(zs)], BF16)
+    part = add_parts((packed, swap(packed, 2)), F32)
     arrived = []
     place = 0
     for index, group in enumerate(groups):
-        shapes = [jax.ShapeDtypeStruct((width, side), BF16 if z else F32) for z in group]
-        args = [*keeps[place : place + len(group)], from_y[index]]
-        if index != 1:
-            shapes.append(half)
-            args += [part, swap(part, bits.pop(0))]
-        if index == 2:
-            args.insert(0, summed[0])
-        *summed, = call(
-            functools.partial(join_kernel, len(group), index == 2),
-            shapes,
-            args,
+        summed = call(
+            functools.partial(join_kernel, len(group)),
+            [jax.ShapeDtypeStruct((width, side), BF16 if z else F32) for z in group],
+            [*keeps[place : place + len(group)], from_y[index]],
             flops=len(group) * side * width,
-            in_specs=[pl.BlockSpec(memory_space=pl.ANY)] * (index == 2) + [VMEM] * (len(args) - (index == 2)),
-            moved=JOIN,
+            moved=len(group) * side * width * 8,
         )
-        if index != 1:
-            part = summed.pop()
         arrived += [swap(piece, z) if z else piece for piece, z in zip(summed, group)]
         place += len(group)
-    for bit in bits:
-        part = part + swap(part, bit)
     part_other = swap(part[: width // 2], 1)
     grad_features, grad_weight, grad_bias = call(
         finish_kernel,

time: 64.8 us -> 56.6 us (0.87)
  waiting for transfers between devices: 25 us -> 10.1 us
  starting transfers between devices: 26.9 us -> 31.1 us
  Pallas kernels: 10.5 us -> 13 us
    ppermute x28 -> x30, waiting for transfers between devices: 25 us -> 10.1 us  [swap(): return lax.ppermute(x, 'row', [(i, i ^ bit) for i in range(count)])]
    ppermute x28 -> x30, starting transfers between devices: 26.9 us -> 31.1 us  [swap(): return lax.ppermute(x, 'row', [(i, i ^ bit) for i in range(count)])]
    pallas_call x10 -> x14, Pallas kernels: 10.5 us -> 13 us  [call(): pl.pallas_call(kernel, out_shape=out_shape, in_specs=in_specs or [VMEM] *...]
  transfers between devices with their start and end apart: 28 -> 30, of which waited for: 8 -> 7; matrix products, arithmetic and copies ran while one was open for 0% -> 0% of each run, Pallas kernels for 12% -> 18%
where the time goes in v3:
time: 56.6 us; the launch traced here: 56.4 us
  starting transfers between devices  31.1 us (55%)
  Pallas kernels  13 us (23%)
  waiting for transfers between devices  10.1 us (18%)
  between operations  1.51 us (3%)
  local copies, waits for them, and re-layouts  0.68 us (1%)
    ppermute x30, starting transfers between devices, swap(): return lax.ppermute(x, 'row', [(i, i ^ bit) for i in range(count)])  31.1 us
    pallas_call x14, Pallas kernels, call(): pl.pallas_call(kernel, out_shape=out_shape, in_specs=in_specs or [VMEM] *...  13 us
    ppermute x30, waiting for transfers between devices, swap(): return lax.ppermute(x, 'row', [(i, i ^ bit) for i in range(count)])  10.1 us
  transfers between devices with their start and end apart: 30, of which 7 were waited for; matrix products, arithmetic and copies ran while one was open for 0% of the time, Pallas kernels for 18%

profile of v3, /device:TPU:0, one launch (start us, length us, event | category | flops | bytes accessed | tf_op | source)
XLA Modules:
  0.0 56.4 jit_solution(4653144277998496240)
XLA Ops:
  0.6 4.1 %collective-permute-start.11 = (bf16[256,256]{1,0:T(8,128)(2,1)}, bf16[256,256]{1,0:T(8,128)(2,1)S(1)}, u32[]{:S(2)}, u32[]{:S(2)}) collective-permute-start(bf16[256,256]{1,0:T(8,128)(2,1)} %refs_8_.1), channel_id=1, source_target_pairs={{0,8},{1,9},{2,10},{3,11},{4,12},{5,13},{6,14},{7,15},{8,0},{9,1},... | collective-permute-start | bytes 393224 | tf_op jit(solution)/shard_map/ppermute | solution.py:191
  4.7 1.6 %collective-permute-start.9 = (bf16[256,256]{1,0:T(8,128)(2,1)}, bf16[256,256]{1,0:T(8,128)(2,1)S(1)}, u32[]{:S(2)}, u32[]{:S(2)}) collective-permute-start(bf16[256,256]{1,0:T(8,128)(2,1)} %refs_8_.1), channel_id=1, source_target_pairs={{0,4},{1,5},{2,6},{3,7},{4,0},{5,1},{6,2},{7,3},{8,12},{9,13},{10,... | collective-permute-start | bytes 393224 | tf_op jit(solution)/shard_map/ppermute | solution.py:191
  6.3 1.5 %collective-permute-start.8 = (bf16[256,256]{1,0:T(8,128)(2,1)}, bf16[256,256]{1,0:T(8,128)(2,1)S(1)}, u32[]{:S(2)}, u32[]{:S(2)}) collective-permute-start(bf16[256,256]{1,0:T(8,128)(2,1)} %refs_8_.1), channel_id=1, source_target_pairs={{0,2},{1,3},{2,0},{3,1},{4,6},{5,7},{6,4},{7,5},{8,10},{9,11},{10,... | collective-permute-start | bytes 393224 | tf_op jit(solution)/shard_map/ppermute | solution.py:191
  7.8 0.2 collective-permute-start.13
  8.7 0.6 %copy-done.3 = s32[1,64]{1,0:T(1,128)S(1)} copy-done((s32[1,64]{1,0:T(1,128)S(1)}, s32[1,64]{1,0:T(1,128)}, u32[]{:S(2)}) %copy-start.3) | copy-done | bytes 280
  9.4 4.6 %shard_map.103 = (bf16[1,256,256]{2,1,0:T(8,128)(2,1)S(1)}, bf16[1,256,256]{2,1,0:T(8,128)(2,1)S(1)}, bf16[1,256,256]{2,1,0:T(8,128)(2,1)S(1)}, bf16[1,256,256]{...) custom-call(s32[64]{0:T(128)S(1)} %bitcast.5, ...), custom_call_target="tpu_custom_call" | custom-call | flops 4194304 | bytes 4194304 | tf_op jit(solution)/shard_map/pallas_call | solution.py:34
  13.9 0.0 copy-start
  14.0 0.0 copy-start.2
  14.0 0.0 copy-start.4
  14.0 0.1 collective-permute-start
  14.1 0.5 collective-permute-start.1
  14.6 0.1 collective-permute-start.2
  14.7 0.4 collective-permute-start.3
  15.1 0.2 collective-permute-done.13.refs_14_
  15.3 0.1 collective-permute-done.refs_0_
  15.4 0.4 collective-permute-start.5
  15.8 0.1 collective-permute-start.6
  15.9 0.0 collective-permute-done.2.refs_2_
  15.9 0.4 collective-permute-start.7
  16.3 1.5 %collective-permute-start.12 = (bf16[256,256]{1,0:T(8,128)(2,1)S(1)}, bf16[256,256]{1,0:T(8,128)(2,1)S(1)}, u32[]{:S(2)}, u32[]{:S(2)}) collective-permute-start(bf16[256,256]{1,0:T(8,128)(2,1)S(1)} %collective-permute-done.11.refs_12_), channel_id=1, source_target_pairs={{0,2},{1,3},{2,0},{3,1},{4,6},{5,7},{6,4},{7,5},{8,10},{9,11},{10,... | collective-permute-start | bytes 393224 | tf_op jit(solution)/shard_map/ppermute | solution.py:191
  17.8 2.4 %collective-permute-start.10 = (bf16[256,256]{1,0:T(8,128)(2,1)S(1)}, bf16[256,256]{1,0:T(8,128)(2,1)S(1)}, u32[]{:S(2)}, u32[]{:S(2)}) collective-permute-start(bf16[256,256]{1,0:T(8,128)(2,1)S(1)} %collective-permute-done.8.refs_9_), channel_id=1, source_target_pairs={{0,4},{1,5},{2,6},{3,7},{4,0},{5,1},{6,2},{7,3},{8,12},{9,13},{10,... | collective-permute-start | bytes 393224 | tf_op jit(solution)/shard_map/ppermute | solution.py:191
  20.3 0.5 collective-permute-start.14
  20.8 4.6 %shard_map.102.own = bf16[8,256,256]{2,1,0:T(8,128)(2,1)S(1)} custom-call(s32[64]{0:T(128)S(1)} %bitcast.6, s32[1]{0:T(128)S(6)} %copy.11.live, s32[1]{0:T(128)} %bitcast.1.me, bf16[64,256,256]{2,1,0:T(8,128)(2,1)} %tiles.3), custom_call_target="tpu_custom_call" | custom-call | flops 4194304 | bytes 4194304 | tf_op jit(solution)/shard_map/pallas_call | solution.py:34
  25.5 0.7 %shard_map.104 = (f32[256,256]{1,0:T(8,128)S(1)}, f32[256,256]{1,0:T(8,128)S(1)}) custom-call(bf16[8,256,256]{2,1,0:T(8,128)(2,1)S(1)} %shard_map.102.own, bf16[1,256,256]{2,1,0:T(8,128)(2,1)S(1)} %collective-permute-done.refs_0_, bf16[1,256,256]{2,1,0:T(8,128)(2,1)S(1)} %collective-permute-done.1.refs_1_, ...), custom_call_target="tpu_custom_call" | custom-call | flops 536870912 | bytes 3145728 | tf_op jit(solution)/shard_map/pallas_call | solution.py:34
  26.2 0.1 collective-permute-start.15
  26.3 1.5 %collective-permute-done.15.received = f32[256,256]{1,0:T(8,128)S(1)} collective-permute-done((f32[256,256]{1,0:T(8,128)S(1)}, f32[256,256]{1,0:T(8,128)S(1)}, u32[]{:S(2)}, u32[]{:S(2)}) %collective-permute-start.15) | collective-permute-done | bytes 262176 | tf_op jit(solution)/shard_map/ppermute | solution.py:191
  27.8 1.0 %shard_map.105 = (bf16[256,256]{1,0:T(8,128)(2,1)}, bf16[256,256]{1,0:T(8,128)(2,1)S(1)}, f32[8,256]{1,0:T(8,128)S(1)}) custom-call(f32[256,256]{1,0:T(8,128)S(1)} %get-tuple-element.38.mine, f32[256,256]{1,0:T(8,128)S(1)} %collective-permute-done.15.received, bf16[256,256]{1,0:T(8,128)(2,1)S(1)} %copy-done, f32[1,256]{1,0:T(1,128)S(1)} %bitcast.7, ...), custom_call_target="tpu_custom_call" | custom-call | flops 67108864 | bytes 1048576 | tf_op jit(solution)/shard_map/pallas_call | solution.py:34
  28.7 0.1 collective-permute-start.16
  28.9 0.3 shard_map.111
  29.2 0.4 collective-permute-start.24
  29.6 0.5 collective-permute-done.16.grad_other
  30.1 0.7 %shard_map.106 = (bf16[1,256,256]{2,1,0:T(8,128)(2,1)S(1)}, bf16[1,256,256]{2,1,0:T(8,128)(2,1)S(1)}, bf16[1,256,256]{2,1,0:T(8,128)(2,1)S(1)}, bf16[1,256,256]{...) custom-call(bf16[8,256,256]{2,1,0:T(8,128)(2,1)S(1)} %shard_map.102., ...), custom_call_target="tpu_custom_call" | custom-call | flops 536870912 | bytes 3145728 | tf_op jit(solution)/shard_map/pallas_call | solution.py:34
  30.9 3.4 %collective-permute-start.27 = (bf16[144,256]{1,0:T(8,128)(2,1)S(1)}, bf16[144,256]{1,0:T(8,128)(2,1)S(1)}, u32[]{:S(2)}, u32[]{:S(2)}) collective-permute-start(bf16[144,256]{1,0:T(8,128)(2,1)S(1)} %shard_map.112.refs_0_), channel_id=1, source_target_pairs={{0,12},{1,13},{2,14},{3,15},{4,8},{5,9},{6,10},{7,11},{8,4},{9,5},... | collective-permute-start | bytes 221192 | tf_op jit(solution)/shard_map/ppermute | solution.py:191
  34.3 0.1 collective-permute-start.26
  34.3 1.0 %collective-permute-start.25 = (bf16[144,256]{1,0:T(8,128)(2,1)S(1)}, bf16[144,256]{1,0:T(8,128)(2,1)S(1)}, u32[]{:S(2)}, u32[]{:S(2)}) collective-permute-start(bf16[144,256]{1,0:T(8,128)(2,1)S(1)} %shard_map.112.refs_0_), channel_id=1, source_target_pairs={{0,4},{1,5},{2,6},{3,7},{4,0},{5,1},{6,2},{7,3},{8,12},{9,13},{10,... | collective-permute-start | bytes 221192 | tf_op jit(solution)/shard_map/ppermute | solution.py:191
  35.3 1.1 %collective-permute-start.20 = (bf16[1,256,256]{2,1,0:T(8,128)(2,1)S(1)}, bf16[1,256,256]{2,1,0:T(8,128)(2,1)S(1)}, u32[]{:S(2)}, u32[]{:S(2)}) collective-permute-start(bf16[1,256,256]{2,1,0:T(8,128)(2,1)S(1)} %get-tuple-element.47), channel_id=1, source_target_pairs={{0,2},{1,3},{2,0},{3,1},{4,6},{5,7},{6,4},{7,5},{8,10},{9,11},{10,... | collective-permute-start | bytes 393224 | tf_op jit(solution)/shard_map/ppermute | solution.py:191
  36.4 1.0 %collective-permute-start.22 = (bf16[1,256,256]{2,1,0:T(8,128)(2,1)S(1)}, bf16[1,256,256]{2,1,0:T(8,128)(2,1)S(1)}, u32[]{:S(2)}, u32[]{:S(2)}) collective-permute-start(bf16[1,256,256]{2,1,0:T(8,128)(2,1)S(1)} %get-tuple-element.49), channel_id=1, source_target_pairs={{0,2},{1,3},{2,0},{3,1},{4,6},{5,7},{6,4},{7,5},{8,10},{9,11},{10,... | collective-permute-start | bytes 393224 | tf_op jit(solution)/shard_map/ppermute | solution.py:191
  37.3 1.1 %collective-permute-start.18 = (bf16[1,256,256]{2,1,0:T(8,128)(2,1)S(1)}, bf16[1,256,256]{2,1,0:T(8,128)(2,1)S(1)}, u32[]{:S(2)}, u32[]{:S(2)}) collective-permute-start(bf16[1,256,256]{2,1,0:T(8,128)(2,1)S(1)} %get-tuple-element.45.refs_2_), channel_id=1, source_target_pairs={{0,2},{1,3},{2,0},{3,1},{4,6},{5,7},{6,4},{7,5},{8,10},{9,11},{10,... | collective-permute-start | bytes 393224 | tf_op jit(solution)/shard_map/ppermute | solution.py:191
  38.4 3.3 %collective-permute-done.26.refs_2_ = bf16[144,256]{1,0:T(8,128)(2,1)S(1)} collective-permute-done((bf16[144,256]{1,0:T(8,128)(2,1)S(1)}, bf16[144,256]{1,0:T(8,128)(2,1)S(1)}, u32[]{:S(2)}, u32[]{:S(2)}) %collective-permute-start.26) | collective-permute-done | bytes 73760 | tf_op jit(solution)/shard_map/ppermute | solution.py:191
  41.7 1.4 %collective-permute-start.28 = (bf16[144,256]{1,0:T(8,128)(2,1)S(1)}, bf16[144,256]{1,0:T(8,128)(2,1)S(1)}, u32[]{:S(2)}, u32[]{:S(2)}) collective-permute-start(bf16[144,256]{1,0:T(8,128)(2,1)S(1)} %shard_map.113.refs_0_), channel_id=1, source_target_pairs={{0,2},{1,3},{2,0},{3,1},{4,6},{5,7},{6,4},{7,5},{8,10},{9,11},{10,... | collective-permute-start | bytes 221192 | tf_op jit(solution)/shard_map/ppermute | solution.py:191
  43.1 0.7 %collective-permute-start.17 = (bf16[1,256,256]{2,1,0:T(8,128)(2,1)S(1)}, bf16[1,256,256]{2,1,0:T(8,128)(2,1)S(1)}, u32[]{:S(2)}, u32[]{:S(2)}) collective-permute-start(bf16[1,256,256]{2,1,0:T(8,128)(2,1)S(1)} %get-tuple-element.43), channel_id=1, source_target_pairs={{0,2},{1,3},{2,0},{3,1},{4,6},{5,7},{6,4},{7,5},{8,10},{9,11},{10,... | collective-permute-start | bytes 393224 | tf_op jit(solution)/shard_map/ppermute | solution.py:191
  43.8 2.5 %collective-permute-start.21 = (bf16[256,256]{1,0:T(8,128)(2,1)S(1)}, bf16[256,256]{1,0:T(8,128)(2,1)S(1)}, u32[]{:S(2)}, u32[]{:S(2)}) collective-permute-start(bf16[256,256]{1,0:T(8,128)(2,1)S(1)} %shard_map.109), channel_id=1, source_target_pairs={{0,8},{1,9},{2,10},{3,11},{4,12},{5,13},{6,14},{7,15},{8,0},{9,1},... | collective-permute-start | bytes 393224 | tf_op jit(solution)/shard_map/ppermute | solution.py:191
  46.3 0.9 %collective-permute-start.23 = (bf16[256,256]{1,0:T(8,128)(2,1)S(1)}, bf16[256,256]{1,0:T(8,128)(2,1)S(1)}, u32[]{:S(2)}, u32[]{:S(2)}) collective-permute-start(bf16[256,256]{1,0:T(8,128)(2,1)S(1)} %shard_map.110), channel_id=1, source_target_pairs={{0,4},{1,5},{2,6},{3,7},{4,0},{5,1},{6,2},{7,3},{8,12},{9,13},{10,... | collective-permute-start | bytes 393224 | tf_op jit(solution)/shard_map/ppermute | solution.py:191
  47.2 3.6 %collective-permute-start.19 = (bf16[256,256]{1,0:T(8,128)(2,1)S(1)}, bf16[256,256]{1,0:T(8,128)(2,1)S(1)}, u32[]{:S(2)}, u32[]{:S(2)}) collective-permute-start(bf16[256,256]{1,0:T(8,128)(2,1)S(1)} %shard_map.108), channel_id=1, source_target_pairs={{0,12},{1,13},{2,14},{3,15},{4,8},{5,9},{6,10},{7,11},{8,4},{9,5},... | collective-permute-start | bytes 393224 | tf_op jit(solution)/shard_map/ppermute | solution.py:191
  50.9 0.1 collective-permute-start.29
  51.0 4.4 %collective-permute-done.21.refs_1_ = bf16[256,256]{1,0:T(8,128)(2,1)S(1)} collective-permute-done((bf16[256,256]{1,0:T(8,128)(2,1)S(1)}, bf16[256,256]{1,0:T(8,128)(2,1)S(1)}, u32[]{:S(2)}, u32[]{:S(2)}) %collective-permute-start.21) | collective-permute-done | bytes 131104 | tf_op jit(solution)/shard_map/ppermute | solution.py:191
  55.4 0.1 collective-permute-done.23.refs_2_
  55.5 0.9 %shard_map.115 = (bf16[256,256]{1,0:T(8,128)(2,1)}, f32[256,256]{1,0:T(8,128)}, f32[1,256]{1,0:T(1,128)}) custom-call(s32[1]{0:T(128)} %bitcast.3.core, f32[256,256]{1,0:T(8,128)S(1)} %shard_map.107.kept, bf16[256,256]{1,0:T(8,128)(2,1)S(1)} %collective-permute-done.19.refs_0_, bf16[256,256]{1,0:T(8,128)(2,1)S(1)} %collective-permute-done.21.refs_1_, ...), custom_call_target="tpu_custom_call" | custom-call | flops 33554432 | bytes 1048576 | tf_op jit(solution)/shard_map/pallas_call | solution.py:34
  (37 shorter events, 0.3 us)
Async XLA Ops:
  0.6 13.4 %collective-permute-start.11 = (bf16[256,256]{1,0:T(8,128)(2,1)}, bf16[256,256]{1,0:T(8,128)(2,1)S(1)}, u32[]{:S(2)}, u32[]{:S(2)}) collective-permute-start(bf16[256,256]{1,0:T(8,128)(2,1)} %refs_8_.1), channel_id=1, source_target_pairs={{0,8},{1,9},{2,10},{3,11},{4,12},{5,13},{6,14},{7,15},{8,0},{9,1},... | collective-permute-start | bytes 393224 | tf_op jit(solution)/shard_map/ppermute | solution.py:191
  4.7 9.8 %collective-permute-start.9 = (bf16[256,256]{1,0:T(8,128)(2,1)}, bf16[256,256]{1,0:T(8,128)(2,1)S(1)}, u32[]{:S(2)}, u32[]{:S(2)}) collective-permute-start(bf16[256,256]{1,0:T(8,128)(2,1)} %refs_8_.1), channel_id=1, source_target_pairs={{0,4},{1,5},{2,6},{3,7},{4,0},{5,1},{6,2},{7,3},{8,12},{9,13},{10,... | collective-permute-start | bytes 393224 | tf_op jit(solution)/shard_map/ppermute | solution.py:191
  6.3 8.3 %collective-permute-start.8 = (bf16[256,256]{1,0:T(8,128)(2,1)}, bf16[256,256]{1,0:T(8,128)(2,1)S(1)}, u32[]{:S(2)}, u32[]{:S(2)}) collective-permute-start(bf16[256,256]{1,0:T(8,128)(2,1)} %refs_8_.1), channel_id=1, source_target_pairs={{0,2},{1,3},{2,0},{3,1},{4,6},{5,7},{6,4},{7,5},{8,10},{9,11},{10,... | collective-permute-start | bytes 393224 | tf_op jit(solution)/shard_map/ppermute | solution.py:191
  7.8 7.4 %collective-permute-start.13 = (bf16[256,256]{1,0:T(8,128)(2,1)}, bf16[256,256]{1,0:T(8,128)(2,1)S(1)}, u32[]{:S(2)}, u32[]{:S(2)}) collective-permute-start(bf16[256,256]{1,0:T(8,128)(2,1)} %refs_8_.1), channel_id=1, source_target_pairs={{0,12},{1,13},{2,14},{3,15},{4,8},{5,9},{6,10},{7,11},{8,4},{9,5},... | collective-permute-start | bytes 393224 | tf_op jit(solution)/shard_map/ppermute | solution.py:191
  8.7 0.7 %copy-start.3 = (s32[1,64]{1,0:T(1,128)S(1)}, s32[1,64]{1,0:T(1,128)}, u32[]{:S(2)}) copy-start(s32[1,64]{1,0:T(1,128)} %param.11) | copy-start | bytes 772
  9.4 16.1 %copy-start.1 = (bf16[256,256]{1,0:T(8,128)(2,1)S(1)}, bf16[256,256]{1,0:T(8,128)(2,1)}, u32[]{:S(2)}) copy-start(bf16[256,256]{1,0:T(8,128)(2,1)} %refs_8_.1) | copy-start | bytes 393220
  13.9 13.8 %copy-start = (bf16[256,256]{1,0:T(8,128)(2,1)S(1)}, bf16[256,256]{1,0:T(8,128)(2,1)}, u32[]{:S(2)}) copy-start(bf16[256,256]{1,0:T(8,128)(2,1)} %refs_3_.1) | copy-start | bytes 393220
  14.0 13.8 %copy-start.2 = (bf16[256,256]{1,0:T(8,128)(2,1)S(1)}, bf16[256,256]{1,0:T(8,128)(2,1)}, u32[]{:S(2)}) copy-start(bf16[256,256]{1,0:T(8,128)(2,1)} %cotangent.1) | copy-start | bytes 393220
  14.0 13.8 %copy-start.4 = (f32[256]{0:T(256)S(1)}, f32[256]{0:T(256)}, u32[]{:S(2)}) copy-start(f32[256]{0:T(256)} %param.9) | copy-start | bytes 3076
  14.0 1.4 %collective-permute-start = (bf16[1,256,256]{2,1,0:T(8,128)(2,1)S(1)}, bf16[1,256,256]{2,1,0:T(8,128)(2,1)S(1)}, u32[]{:S(2)}, u32[]{:S(2)}) collective-permute-start(bf16[1,256,256]{2,1,0:T(8,128)(2,1)S(1)} %get-tuple-element.30), channel_id=1, source_target_pairs={{0,1},{1,0},{2,3},{3,2},{4,5},{5,4},{6,7},{7,6},{8,9},{9,8},{10,11... | collective-permute-start | bytes 393224 | tf_op jit(solution)/shard_map/ppermute | solution.py:191
  14.1 1.7 %collective-permute-start.1 = (bf16[1,256,256]{2,1,0:T(8,128)(2,1)S(1)}, bf16[1,256,256]{2,1,0:T(8,128)(2,1)S(1)}, u32[]{:S(2)}, u32[]{:S(2)}) collective-permute-start(bf16[1,256,256]{2,1,0:T(8,128)(2,1)S(1)} %get-tuple-element.31), channel_id=1, source_target_pairs={{0,1},{1,0},{2,3},{3,2},{4,5},{5,4},{6,7},{7,6},{8,9},{9,8},{10,11... | collective-permute-start | bytes 393224 | tf_op jit(solution)/shard_map/ppermute | solution.py:191
  14.6 1.3 %collective-permute-start.2 = (bf16[1,256,256]{2,1,0:T(8,128)(2,1)S(1)}, bf16[1,256,256]{2,1,0:T(8,128)(2,1)S(1)}, u32[]{:S(2)}, u32[]{:S(2)}) collective-permute-start(bf16[1,256,256]{2,1,0:T(8,128)(2,1)S(1)} %get-tuple-element.32), channel_id=1, source_target_pairs={{0,1},{1,0},{2,3},{3,2},{4,5},{5,4},{6,7},{7,6},{8,9},{9,8},{10,11... | collective-permute-start | bytes 393224 | tf_op jit(solution)/shard_map/ppermute | solution.py:191
  14.7 1.6 %collective-permute-start.3 = (bf16[1,256,256]{2,1,0:T(8,128)(2,1)S(1)}, bf16[1,256,256]{2,1,0:T(8,128)(2,1)S(1)}, u32[]{:S(2)}, u32[]{:S(2)}) collective-permute-start(bf16[1,256,256]{2,1,0:T(8,128)(2,1)S(1)} %get-tuple-element.33), channel_id=1, source_target_pairs={{0,1},{1,0},{2,3},{3,2},{4,5},{5,4},{6,7},{7,6},{8,9},{9,8},{10,11... | collective-permute-start | bytes 393224 | tf_op jit(solution)/shard_map/ppermute | solution.py:191
  15.3 2.6 %collective-permute-start.4 = (bf16[1,256,256]{2,1,0:T(8,128)(2,1)S(1)}, bf16[1,256,256]{2,1,0:T(8,128)(2,1)S(1)}, u32[]{:S(2)}, u32[]{:S(2)}) collective-permute-start(bf16[1,256,256]{2,1,0:T(8,128)(2,1)S(1)} %get-tuple-element.34), channel_id=1, source_target_pairs={{0,1},{1,0},{2,3},{3,2},{4,5},{5,4},{6,7},{7,6},{8,9},{9,8},{10,11... | collective-permute-start | bytes 393224 | tf_op jit(solution)/shard_map/ppermute | solution.py:191
  15.4 4.9 %collective-permute-start.5 = (bf16[1,256,256]{2,1,0:T(8,128)(2,1)S(1)}, bf16[1,256,256]{2,1,0:T(8,128)(2,1)S(1)}, u32[]{:S(2)}, u32[]{:S(2)}) collective-permute-start(bf16[1,256,256]{2,1,0:T(8,128)(2,1)S(1)} %get-tuple-element.35), channel_id=1, source_target_pairs={{0,1},{1,0},{2,3},{3,2},{4,5},{5,4},{6,7},{7,6},{8,9},{9,8},{10,11... | collective-permute-start | bytes 393224 | tf_op jit(solution)/shard_map/ppermute | solution.py:191
  15.8 9.6 %collective-permute-start.6 = (bf16[1,256,256]{2,1,0:T(8,128)(2,1)S(1)}, bf16[1,256,256]{2,1,0:T(8,128)(2,1)S(1)}, u32[]{:S(2)}, u32[]{:S(2)}) collective-permute-start(bf16[1,256,256]{2,1,0:T(8,128)(2,1)S(1)} %get-tuple-element.36), channel_id=1, source_target_pairs={{0,1},{1,0},{2,3},{3,2},{4,5},{5,4},{6,7},{7,6},{8,9},{9,8},{10,11... | collective-permute-start | bytes 393224 | tf_op jit(solution)/shard_map/ppermute | solution.py:191
  15.9 9.5 %collective-permute-start.7 = (bf16[1,256,256]{2,1,0:T(8,128)(2,1)S(1)}, bf16[1,256,256]{2,1,0:T(8,128)(2,1)S(1)}, u32[]{:S(2)}, u32[]{:S(2)}) collective-permute-start(bf16[1,256,256]{2,1,0:T(8,128)(2,1)S(1)} %get-tuple-element.37), channel_id=1, source_target_pairs={{0,1},{1,0},{2,3},{3,2},{4,5},{5,4},{6,7},{7,6},{8,9},{9,8},{10,11... | collective-permute-start | bytes 393224 | tf_op jit(solution)/shard_map/ppermute | solution.py:191
  16.3 9.1 %collective-permute-start.12 = (bf16[256,256]{1,0:T(8,128)(2,1)S(1)}, bf16[256,256]{1,0:T(8,128)(2,1)S(1)}, u32[]{:S(2)}, u32[]{:S(2)}) collective-permute-start(bf16[256,256]{1,0:T(8,128)(2,1)S(1)} %collective-permute-done.11.refs_12_), channel_id=1, source_target_pairs={{0,2},{1,3},{2,0},{3,1},{4,6},{5,7},{6,4},{7,5},{8,10},{9,11},{10,... | collective-permute-start | bytes 393224 | tf_op jit(solution)/shard_map/ppermute | solution.py:191
  17.8 7.6 %collective-permute-start.10 = (bf16[256,256]{1,0:T(8,128)(2,1)S(1)}, bf16[256,256]{1,0:T(8,128)(2,1)S(1)}, u32[]{:S(2)}, u32[]{:S(2)}) collective-permute-start(bf16[256,256]{1,0:T(8,128)(2,1)S(1)} %collective-permute-done.8.refs_9_), channel_id=1, source_target_pairs={{0,4},{1,5},{2,6},{3,7},{4,0},{5,1},{6,2},{7,3},{8,12},{9,13},{10,... | collective-permute-start | bytes 393224 | tf_op jit(solution)/shard_map/ppermute | solution.py:191
  20.3 5.2 %collective-permute-start.14 = (bf16[256,256]{1,0:T(8,128)(2,1)S(1)}, bf16[256,256]{1,0:T(8,128)(2,1)S(1)}, u32[]{:S(2)}, u32[]{:S(2)}) collective-permute-start(bf16[256,256]{1,0:T(8,128)(2,1)S(1)} %collective-permute-done.13.refs_14_), channel_id=1, source_target_pairs={{0,2},{1,3},{2,0},{3,1},{4,6},{5,7},{6,4},{7,5},{8,10},{9,11},{10,... | collective-permute-start | bytes 393224 | tf_op jit(solution)/shard_map/ppermute | solution.py:191
  26.2 1.6 %collective-permute-start.15 = (f32[256,256]{1,0:T(8,128)S(1)}, f32[256,256]{1,0:T(8,128)S(1)}, u32[]{:S(2)}, u32[]{:S(2)}) collective-permute-start(f32[256,256]{1,0:T(8,128)S(1)} %get-tuple-element.39), channel_id=1, source_target_pairs={{0,1},{1,0},{2,3},{3,2},{4,5},{5,4},{6,7},{7,6},{8,9},{9,8},{10,11... | collective-permute-start | bytes 786440 | tf_op jit(solution)/shard_map/ppermute | solution.py:191
  28.7 1.3 %collective-permute-start.16 = (bf16[256,256]{1,0:T(8,128)(2,1)S(1)}, bf16[256,256]{1,0:T(8,128)(2,1)S(1)}, u32[]{:S(2)}, u32[]{:S(2)}) collective-permute-start(bf16[256,256]{1,0:T(8,128)(2,1)S(1)} %get-tuple-element.41.grad), channel_id=1, source_target_pairs={{0,1},{1,0},{2,3},{3,2},{4,5},{5,4},{6,7},{7,6},{8,9},{9,8},{10,11... | collective-permute-start | bytes 393224 | tf_op jit(solution)/shard_map/ppermute | solution.py:191
  29.2 1.6 %collective-permute-start.24 = (f32[144,256]{1,0:T(8,128)S(1)}, f32[144,256]{1,0:T(8,128)S(1)}, u32[]{:S(2)}, u32[]{:S(2)}) collective-permute-start(f32[144,256]{1,0:T(8,128)S(1)} %get-tuple-element.52), channel_id=1, source_target_pairs={{0,1},{1,0},{2,3},{3,2},{4,5},{5,4},{6,7},{7,6},{8,9},{9,8},{10,11... | collective-permute-start | bytes 442376 | tf_op jit(solution)/shard_map/ppermute | solution.py:191
  30.9 6.5 %collective-permute-start.27 = (bf16[144,256]{1,0:T(8,128)(2,1)S(1)}, bf16[144,256]{1,0:T(8,128)(2,1)S(1)}, u32[]{:S(2)}, u32[]{:S(2)}) collective-permute-start(bf16[144,256]{1,0:T(8,128)(2,1)S(1)} %shard_map.112.refs_0_), channel_id=1, source_target_pairs={{0,12},{1,13},{2,14},{3,15},{4,8},{5,9},{6,10},{7,11},{8,4},{9,5},... | collective-permute-start | bytes 221192 | tf_op jit(solution)/shard_map/ppermute | solution.py:191
  34.3 7.4 %collective-permute-start.26 = (bf16[144,256]{1,0:T(8,128)(2,1)S(1)}, bf16[144,256]{1,0:T(8,128)(2,1)S(1)}, u32[]{:S(2)}, u32[]{:S(2)}) collective-permute-start(bf16[144,256]{1,0:T(8,128)(2,1)S(1)} %shard_map.112.refs_0_), channel_id=1, source_target_pairs={{0,8},{1,9},{2,10},{3,11},{4,12},{5,13},{6,14},{7,15},{8,0},{9,1},... | collective-permute-start | bytes 221192 | tf_op jit(solution)/shard_map/ppermute | solution.py:191
  34.3 7.3 %collective-permute-start.25 = (bf16[144,256]{1,0:T(8,128)(2,1)S(1)}, bf16[144,256]{1,0:T(8,128)(2,1)S(1)}, u32[]{:S(2)}, u32[]{:S(2)}) collective-permute-start(bf16[144,256]{1,0:T(8,128)(2,1)S(1)} %shard_map.112.refs_0_), channel_id=1, source_target_pairs={{0,4},{1,5},{2,6},{3,7},{4,0},{5,1},{6,2},{7,3},{8,12},{9,13},{10,... | collective-permute-start | bytes 221192 | tf_op jit(solution)/shard_map/ppermute | solution.py:191
  35.3 8.5 %collective-permute-start.20 = (bf16[1,256,256]{2,1,0:T(8,128)(2,1)S(1)}, bf16[1,256,256]{2,1,0:T(8,128)(2,1)S(1)}, u32[]{:S(2)}, u32[]{:S(2)}) collective-permute-start(bf16[1,256,256]{2,1,0:T(8,128)(2,1)S(1)} %get-tuple-element.47), channel_id=1, source_target_pairs={{0,2},{1,3},{2,0},{3,1},{4,6},{5,7},{6,4},{7,5},{8,10},{9,11},{10,... | collective-permute-start | bytes 393224 | tf_op jit(solution)/shard_map/ppermute | solution.py:191
  36.4 9.9 %collective-permute-start.22 = (bf16[1,256,256]{2,1,0:T(8,128)(2,1)S(1)}, bf16[1,256,256]{2,1,0:T(8,128)(2,1)S(1)}, u32[]{:S(2)}, u32[]{:S(2)}) collective-permute-start(bf16[1,256,256]{2,1,0:T(8,128)(2,1)S(1)} %get-tuple-element.49), channel_id=1, source_target_pairs={{0,2},{1,3},{2,0},{3,1},{4,6},{5,7},{6,4},{7,5},{8,10},{9,11},{10,... | collective-permute-start | bytes 393224 | tf_op jit(solution)/shard_map/ppermute | solution.py:191
  37.3 9.9 %collective-permute-start.18 = (bf16[1,256,256]{2,1,0:T(8,128)(2,1)S(1)}, bf16[1,256,256]{2,1,0:T(8,128)(2,1)S(1)}, u32[]{:S(2)}, u32[]{:S(2)}) collective-permute-start(bf16[1,256,256]{2,1,0:T(8,128)(2,1)S(1)} %get-tuple-element.45.refs_2_), channel_id=1, source_target_pairs={{0,2},{1,3},{2,0},{3,1},{4,6},{5,7},{6,4},{7,5},{8,10},{9,11},{10,... | collective-permute-start | bytes 393224 | tf_op jit(solution)/shard_map/ppermute | solution.py:191
  41.7 9.2 %collective-permute-start.28 = (bf16[144,256]{1,0:T(8,128)(2,1)S(1)}, bf16[144,256]{1,0:T(8,128)(2,1)S(1)}, u32[]{:S(2)}, u32[]{:S(2)}) collective-permute-start(bf16[144,256]{1,0:T(8,128)(2,1)S(1)} %shard_map.113.refs_0_), channel_id=1, source_target_pairs={{0,2},{1,3},{2,0},{3,1},{4,6},{5,7},{6,4},{7,5},{8,10},{9,11},{10,... | collective-permute-start | bytes 221192 | tf_op jit(solution)/shard_map/ppermute | solution.py:191
  43.1 7.9 %collective-permute-start.17 = (bf16[1,256,256]{2,1,0:T(8,128)(2,1)S(1)}, bf16[1,256,256]{2,1,0:T(8,128)(2,1)S(1)}, u32[]{:S(2)}, u32[]{:S(2)}) collective-permute-start(bf16[1,256,256]{2,1,0:T(8,128)(2,1)S(1)} %get-tuple-element.43), channel_id=1, source_target_pairs={{0,2},{1,3},{2,0},{3,1},{4,6},{5,7},{6,4},{7,5},{8,10},{9,11},{10,... | collective-permute-start | bytes 393224 | tf_op jit(solution)/shard_map/ppermute | solution.py:191
  43.8 11.6 %collective-permute-start.21 = (bf16[256,256]{1,0:T(8,128)(2,1)S(1)}, bf16[256,256]{1,0:T(8,128)(2,1)S(1)}, u32[]{:S(2)}, u32[]{:S(2)}) collective-permute-start(bf16[256,256]{1,0:T(8,128)(2,1)S(1)} %shard_map.109), channel_id=1, source_target_pairs={{0,8},{1,9},{2,10},{3,11},{4,12},{5,13},{6,14},{7,15},{8,0},{9,1},... | collective-permute-start | bytes 393224 | tf_op jit(solution)/shard_map/ppermute | solution.py:191
  46.3 9.2 %collective-permute-start.23 = (bf16[256,256]{1,0:T(8,128)(2,1)S(1)}, bf16[256,256]{1,0:T(8,128)(2,1)S(1)}, u32[]{:S(2)}, u32[]{:S(2)}) collective-permute-start(bf16[256,256]{1,0:T(8,128)(2,1)S(1)} %shard_map.110), channel_id=1, source_target_pairs={{0,4},{1,5},{2,6},{3,7},{4,0},{5,1},{6,2},{7,3},{8,12},{9,13},{10,... | collective-permute-start | bytes 393224 | tf_op jit(solution)/shard_map/ppermute | solution.py:191
  47.2 8.3 %collective-permute-start.19 = (bf16[256,256]{1,0:T(8,128)(2,1)S(1)}, bf16[256,256]{1,0:T(8,128)(2,1)S(1)}, u32[]{:S(2)}, u32[]{:S(2)}) collective-permute-start(bf16[256,256]{1,0:T(8,128)(2,1)S(1)} %shard_map.108), channel_id=1, source_target_pairs={{0,12},{1,13},{2,14},{3,15},{4,8},{5,9},{6,10},{7,11},{8,4},{9,5},... | collective-permute-start | bytes 393224 | tf_op jit(solution)/shard_map/ppermute | solution.py:191
  50.9 4.6 %collective-permute-start.29 = (f32[128,256]{1,0:T(8,128)S(1)}, f32[128,256]{1,0:T(8,128)S(1)}, u32[]{:S(2)}, u32[]{:S(2)}) collective-permute-start(f32[128,256]{1,0:T(8,128)S(1)} %slice.4), channel_id=1, source_target_pairs={{0,1},{1,0},{2,3},{3,2},{4,5},{5,4},{6,7},{7,6},{8,9},{9,8},{10,11... | collective-permute-start | bytes 393224 | tf_op jit(solution)/shard_map/ppermute | solution.py:191

commit v4 on v3

--- a/solution.py
+++ b/solution.py
@@ -43,8 +43,8 @@
 
 
 def merge_kernel(parity, columns, live, me, tiles, *refs):
-    others, (held, head, following, sems) = refs[:-4], refs[-4:]
-    depth, side = others[0].shape[:2]
+    outs, (head, following) = refs[:-2], refs[-2:]
+    depth, side = outs[0].shape[:2]
     strip = side // 4
 
     def clear(index, carry):
@@ -61,40 +61,22 @@
 
     lax.fori_loop(0, live[0], link, 0)
 
-    def fetch(slot):
-        return pltpu.make_async_copy(tiles.at[slot], held.at[slot], sems.at[slot])
-
-    def chain(index, act):
-        def step(slot):
-            act(fetch(slot))
-            return following[slot]
-
-        lax.while_loop(lambda slot: slot >= 0, step, head[index])
-
-    outs = [(parity + 2 * depth * index, out) for index, out in enumerate(others)]
-
-    def start(base, index, carry):
-        chain(2 * index + base, lambda copy: copy.start())
-        return carry
-
     def fill(base, out, index, carry):
-        chain(2 * index + base, lambda copy: copy.wait())
         for part in range(4):
             rows = pl.ds(part * strip, strip)
 
             def add(state, rows=rows):
                 slot, total = state
-                return following[slot], total + held[slot, rows, :].astype(F32)
+                return following[slot], total + tiles[slot, rows, :].astype(F32)
 
             first = (head[2 * index + base], jnp.zeros((strip, side), F32))
             total = lax.while_loop(lambda state: state[0] >= 0, add, first)[1]
             out[index, rows, :] = total.astype(BF16)
         return carry
 
-    for base, out in outs:
-        lax.fori_loop(0, out.shape[0], functools.partial(start, base), 0)
-    for base, out in outs:
-        lax.fori_loop(0, out.shape[0], functools.partial(fill, base, out), 0)
+    for piece, out in enumerate(outs):
+        base = parity + 2 * depth * piece
+        lax.fori_loop(0, depth, functools.partial(fill, base, out), 0)
 
 
 def aggregate_kernel(own, *refs):
@@ -197,21 +179,17 @@
     gathered = {0: features}
     for z in zs[:-1] + [2]:
         gathered[z] = swap(features, z)
+
     def merge(parity, pieces):
         return call(
             functools.partial(merge_kernel, parity),
             [jax.ShapeDtypeStruct((pairs // pieces, side, side), BF16)] * pieces,
             (tile_col[0], live_tiles, me[None], tiles),
-            in_specs=[SMEM, SMEM, SMEM, pl.BlockSpec(memory_space=pl.ANY)],
-            scratch=[
-                pltpu.VMEM((slots, side, side), BF16),
-                pltpu.SMEM((count,), jnp.int32),
-                pltpu.SMEM((slots,), jnp.int32),
-                pltpu.SemaphoreType.DMA((slots,)),
-            ],
+            in_specs=[SMEM, SMEM, SMEM, VMEM],
+            scratch=[pltpu.SMEM((count,), jnp.int32), pltpu.SMEM((slots,), jnp.int32)],
             flops=slots * side * side,
             moved=slots * side * side,
-            limit=48,
+            limit=20,
         )
 
     (own,) = merge(0, 1)
@@ -273,9 +251,6 @@
     )
     sends, keeps = outs[: len(groups)], outs[len(groups) :]
     from_y = [swap(send, 2) for send in sends]
-    packed = add_parts((part, swap(part_send, 1)), BF16, outs[:1])
-    packed = add_parts([swap(packed, z) if z else packed for z in reversed(zs)], BF16)
-    part = add_parts((packed, swap(packed, 2)), F32)
     arrived = []
     place = 0
     for index, group in enumerate(groups):
@@ -288,6 +263,9 @@
         )
         arrived += [swap(piece, z) if z else piece for piece, z in zip(summed, group)]
         place += len(group)
+    packed = add_parts((part, swap(part_send, 1)), BF16, outs[:1])
+    packed = add_parts([swap(packed, z) if z else packed for z in reversed(zs)], BF16)
+    part = add_parts((packed, swap(packed, 2)), F32, arrived[:2])
     part_other = swap(part[: width // 2], 1)
     grad_features, grad_weight, grad_bias = call(
         finish_kernel,

time: 56.6 us -> 55.3 us (0.977)
  Pallas kernels: 13 us -> 8.06 us
  waiting for transfers between devices: 10.1 us -> 13.9 us
  starting transfers between devices: 31.1 us -> 27.7 us
  local copies, waits for them, and re-layouts: 0.68 us -> 4.06 us
    pallas_call x14, Pallas kernels: 13 us -> 8.06 us  [call(): pl.pallas_call(kernel, out_shape=out_shape, in_specs=in_specs or [VMEM] *...]
    ppermute x30, waiting for transfers between devices: 10.1 us -> 13.9 us  [swap(): return lax.ppermute(x, 'row', [(i, i ^ bit) for i in range(count)])]
    ppermute x30, starting transfers between devices: 31.1 us -> 27.7 us  [swap(): return lax.ppermute(x, 'row', [(i, i ^ bit) for i in range(count)])]
    unnamed x10 -> x12, local copies, waits for them, and re-layouts: 0.67 us -> 4.05 us
  transfers between devices with their start and end apart: 30 -> 30, of which waited for: 7 -> 10; matrix products, arithmetic and copies ran while one was open for 0% -> 0% of each run, Pallas kernels for 18% -> 10%
where the time goes in v4:
time: 55.3 us; the launch traced here: 55.1 us
  starting transfers between devices  27.7 us (50%)
  waiting for transfers between devices  13.9 us (25%)
  Pallas kernels  8.06 us (15%)
  local copies, waits for them, and re-layouts  4.06 us (7%)
  between operations  1.5 us (3%)
    ppermute x30, starting transfers between devices, swap(): return lax.ppermute(x, 'row', [(i, i ^ bit) for i in range(count)])  27.7 us
    ppermute x30, waiting for transfers between devices, swap(): return lax.ppermute(x, 'row', [(i, i ^ bit) for i in range(count)])  13.9 us
    pallas_call x14, Pallas kernels, call(): pl.pallas_call(kernel, out_shape=out_shape, in_specs=in_specs or [VMEM] *...  8.06 us
    unnamed x12, local copies, waits for them, and re-layouts  4.05 us
  transfers between devices with their start and end apart: 30, of which 10 were waited for; matrix products, arithmetic and copies ran while one was open for 0% of the time, Pallas kernels for 10%

profile of v4, /device:TPU:0, one launch (start us, length us, event | category | flops | bytes accessed | tf_op | source)
XLA Modules:
  0.0 55.1 jit_solution(17717984343459468284)
XLA Ops:
  0.6 4.1 %collective-permute-start.11 = (bf16[256,256]{1,0:T(8,128)(2,1)}, bf16[256,256]{1,0:T(8,128)(2,1)S(1)}, u32[]{:S(2)}, u32[]{:S(2)}) collective-permute-start(bf16[256,256]{1,0:T(8,128)(2,1)} %refs_8_.1), channel_id=1, source_target_pairs={{0,8},{1,9},{2,10},{3,11},{4,12},{5,13},{6,14},{7,15},{8,0},{9,1},... | collective-permute-start | bytes 393224 | tf_op jit(solution)/shard_map/ppermute | solution.py:173
  4.7 1.6 %collective-permute-start.9 = (bf16[256,256]{1,0:T(8,128)(2,1)}, bf16[256,256]{1,0:T(8,128)(2,1)S(1)}, u32[]{:S(2)}, u32[]{:S(2)}) collective-permute-start(bf16[256,256]{1,0:T(8,128)(2,1)} %refs_8_.1), channel_id=1, source_target_pairs={{0,4},{1,5},{2,6},{3,7},{4,0},{5,1},{6,2},{7,3},{8,12},{9,13},{10,... | collective-permute-start | bytes 393224 | tf_op jit(solution)/shard_map/ppermute | solution.py:173
  6.3 1.5 %collective-permute-start.8 = (bf16[256,256]{1,0:T(8,128)(2,1)}, bf16[256,256]{1,0:T(8,128)(2,1)S(1)}, u32[]{:S(2)}, u32[]{:S(2)}) collective-permute-start(bf16[256,256]{1,0:T(8,128)(2,1)} %refs_8_.1), channel_id=1, source_target_pairs={{0,2},{1,3},{2,0},{3,1},{4,6},{5,7},{6,4},{7,5},{8,10},{9,11},{10,... | collective-permute-start | bytes 393224 | tf_op jit(solution)/shard_map/ppermute | solution.py:173
  7.8 0.2 collective-permute-start.13
  8.7 3.4 %copy-done = bf16[64,256,256]{2,1,0:T(8,128)(2,1)S(1)} copy-done((bf16[64,256,256]{2,1,0:T(8,128)(2,1)S(1)}, bf16[64,256,256]{2,1,0:T(8,128)(2,1)}, u32[]{:S(2)}) %copy-start) | copy-done | bytes 8388632
  12.1 0.7 %copy-done.4 = s32[1,64]{1,0:T(1,128)S(1)} copy-done((s32[1,64]{1,0:T(1,128)S(1)}, s32[1,64]{1,0:T(1,128)}, u32[]{:S(2)}) %copy-start.4) | copy-done | bytes 280
  12.7 2.1 %shard_map.103 = (bf16[1,256,256]{2,1,0:T(8,128)(2,1)S(1)}, bf16[1,256,256]{2,1,0:T(8,128)(2,1)S(1)}, bf16[1,256,256]{2,1,0:T(8,128)(2,1)S(1)}, bf16[1,256,256]{...) custom-call(s32[64]{0:T(128)S(1)} %bitcast.5, ...), custom_call_target="tpu_custom_call" | custom-call | flops 4194304 | bytes 4194304 | tf_op jit(solution)/shard_map/pallas_call | solution.py:34
  14.8 0.1 collective-permute-start
  14.9 0.5 collective-permute-start.1
  15.4 0.1 collective-permute-start.2
  15.5 0.4 collective-permute-start.3
  15.9 0.1 collective-permute-start.4
  16.0 0.2 collective-permute-done.refs_0_
  16.3 0.2 collective-permute-start.5
  16.5 0.3 collective-permute-start.6
  16.8 0.2 collective-permute-start.7
  17.0 0.8 %collective-permute-start.12 = (bf16[256,256]{1,0:T(8,128)(2,1)S(1)}, bf16[256,256]{1,0:T(8,128)(2,1)S(1)}, u32[]{:S(2)}, u32[]{:S(2)}) collective-permute-start(bf16[256,256]{1,0:T(8,128)(2,1)S(1)} %collective-permute-done.11.refs_12_), channel_id=1, source_target_pairs={{0,2},{1,3},{2,0},{3,1},{4,6},{5,7},{6,4},{7,5},{8,10},{9,11},{10,... | collective-permute-start | bytes 393224 | tf_op jit(solution)/shard_map/ppermute | solution.py:173
  17.8 2.4 %collective-permute-start.10 = (bf16[256,256]{1,0:T(8,128)(2,1)S(1)}, bf16[256,256]{1,0:T(8,128)(2,1)S(1)}, u32[]{:S(2)}, u32[]{:S(2)}) collective-permute-start(bf16[256,256]{1,0:T(8,128)(2,1)S(1)} %collective-permute-done.8.refs_9_), channel_id=1, source_target_pairs={{0,4},{1,5},{2,6},{3,7},{4,0},{5,1},{6,2},{7,3},{8,12},{9,13},{10,... | collective-permute-start | bytes 393224 | tf_op jit(solution)/shard_map/ppermute | solution.py:173
  20.3 0.5 collective-permute-start.14
  20.8 2.2 %shard_map.102.own = bf16[8,256,256]{2,1,0:T(8,128)(2,1)S(1)} custom-call(s32[64]{0:T(128)S(1)} %bitcast.6, s32[1]{0:T(128)S(6)} %copy.11.live, s32[1]{0:T(128)} %bitcast.1.me, bf16[64,256,256]{2,1,0:T(8,128)(2,1)S(1)} %copy-done), custom_call_target="tpu_custom_call" | custom-call | flops 4194304 | bytes 4194304 | tf_op jit(solution)/shard_map/pallas_call | solution.py:34
  23.0 0.7 %collective-permute-done.10.refs_11_ = bf16[256,256]{1,0:T(8,128)(2,1)S(1)} collective-permute-done((bf16[256,256]{1,0:T(8,128)(2,1)S(1)}, bf16[256,256]{1,0:T(8,128)(2,1)S(1)}, u32[]{:S(2)}, u32[]{:S(2)}) %collective-permute-start.10) | collective-permute-done | bytes 131104 | tf_op jit(solution)/shard_map/ppermute | solution.py:173
  23.7 1.8 %collective-permute-done.14.refs_15_ = bf16[256,256]{1,0:T(8,128)(2,1)S(1)} collective-permute-done((bf16[256,256]{1,0:T(8,128)(2,1)S(1)}, bf16[256,256]{1,0:T(8,128)(2,1)S(1)}, u32[]{:S(2)}, u32[]{:S(2)}) %collective-permute-start.14) | collective-permute-done | bytes 131104 | tf_op jit(solution)/shard_map/ppermute | solution.py:173
  25.5 0.7 %shard_map.104 = (f32[256,256]{1,0:T(8,128)S(1)}, f32[256,256]{1,0:T(8,128)S(1)}) custom-call(bf16[8,256,256]{2,1,0:T(8,128)(2,1)S(1)} %shard_map.102.own, bf16[1,256,256]{2,1,0:T(8,128)(2,1)S(1)} %collective-permute-done.refs_0_, bf16[1,256,256]{2,1,0:T(8,128)(2,1)S(1)} %collective-permute-done.1.refs_1_, ...), custom_call_target="tpu_custom_call" | custom-call | flops 536870912 | bytes 3145728 | tf_op jit(solution)/shard_map/pallas_call | solution.py:34
  26.2 0.1 collective-permute-start.15
  26.3 1.5 %collective-permute-done.15.received = f32[256,256]{1,0:T(8,128)S(1)} collective-permute-done((f32[256,256]{1,0:T(8,128)S(1)}, f32[256,256]{1,0:T(8,128)S(1)}, u32[]{:S(2)}, u32[]{:S(2)}) %collective-permute-start.15) | collective-permute-done | bytes 262176 | tf_op jit(solution)/shard_map/ppermute | solution.py:173
  27.8 1.0 %shard_map.105 = (bf16[256,256]{1,0:T(8,128)(2,1)}, bf16[256,256]{1,0:T(8,128)(2,1)S(1)}, f32[8,256]{1,0:T(8,128)S(1)}) custom-call(f32[256,256]{1,0:T(8,128)S(1)} %get-tuple-element.38.mine, f32[256,256]{1,0:T(8,128)S(1)} %collective-permute-done.15.received, bf16[256,256]{1,0:T(8,128)(2,1)S(1)} %copy-done.1, f32[1,256]{1,0:T(1,128)S(1)} %bitcast.7, ...), custom_call_target="tpu_custom_call" | custom-call | flops 67108864 | bytes 1048576 | tf_op jit(solution)/shard_map/pallas_call | solution.py:34
  28.8 0.1 collective-permute-start.16
  28.9 0.3 shard_map.111
  29.2 0.4 collective-permute-start.24
  29.7 0.4 collective-permute-done.16.grad_other
  30.1 0.7 %shard_map.106 = (bf16[1,256,256]{2,1,0:T(8,128)(2,1)S(1)}, bf16[1,256,256]{2,1,0:T(8,128)(2,1)S(1)}, bf16[1,256,256]{2,1,0:T(8,128)(2,1)S(1)}, bf16[1,256,256]{...) custom-call(bf16[8,256,256]{2,1,0:T(8,128)(2,1)S(1)} %shard_map.102., ...), custom_call_target="tpu_custom_call" | custom-call | flops 536870912 | bytes 3145728 | tf_op jit(solution)/shard_map/pallas_call | solution.py:34
  30.8 0.7 %collective-permute-start.20 = (bf16[1,256,256]{2,1,0:T(8,128)(2,1)S(1)}, bf16[1,256,256]{2,1,0:T(8,128)(2,1)S(1)}, u32[]{:S(2)}, u32[]{:S(2)}) collective-permute-start(bf16[1,256,256]{2,1,0:T(8,128)(2,1)S(1)} %get-tuple-element.47), channel_id=1, source_target_pairs={{0,2},{1,3},{2,0},{3,1},{4,6},{5,7},{6,4},{7,5},{8,10},{9,11},{10,... | collective-permute-start | bytes 393224 | tf_op jit(solution)/shard_map/ppermute | solution.py:173
  31.5 1.4 %collective-permute-start.18 = (bf16[1,256,256]{2,1,0:T(8,128)(2,1)S(1)}, bf16[1,256,256]{2,1,0:T(8,128)(2,1)S(1)}, u32[]{:S(2)}, u32[]{:S(2)}) collective-permute-start(bf16[1,256,256]{2,1,0:T(8,128)(2,1)S(1)} %get-tuple-element.45.refs_2_), channel_id=1, source_target_pairs={{0,2},{1,3},{2,0},{3,1},{4,6},{5,7},{6,4},{7,5},{8,10},{9,11},{10,... | collective-permute-start | bytes 393224 | tf_op jit(solution)/shard_map/ppermute | solution.py:173
  33.0 3.1 %collective-permute-start.27 = (bf16[144,256]{1,0:T(8,128)(2,1)S(1)}, bf16[144,256]{1,0:T(8,128)(2,1)S(1)}, u32[]{:S(2)}, u32[]{:S(2)}) collective-permute-start(bf16[144,256]{1,0:T(8,128)(2,1)S(1)} %shard_map.112.refs_0_), channel_id=1, source_target_pairs={{0,12},{1,13},{2,14},{3,15},{4,8},{5,9},{6,10},{7,11},{8,4},{9,5},... | collective-permute-start | bytes 221192 | tf_op jit(solution)/shard_map/ppermute | solution.py:173
  36.0 0.4 collective-permute-start.26
  36.4 1.0 %collective-permute-start.25 = (bf16[144,256]{1,0:T(8,128)(2,1)S(1)}, bf16[144,256]{1,0:T(8,128)(2,1)S(1)}, u32[]{:S(2)}, u32[]{:S(2)}) collective-permute-start(bf16[144,256]{1,0:T(8,128)(2,1)S(1)} %shard_map.112.refs_0_), channel_id=1, source_target_pairs={{0,4},{1,5},{2,6},{3,7},{4,0},{5,1},{6,2},{7,3},{8,12},{9,13},{10,... | collective-permute-start | bytes 221192 | tf_op jit(solution)/shard_map/ppermute | solution.py:173
  37.4 1.0 %collective-permute-start.22 = (bf16[1,256,256]{2,1,0:T(8,128)(2,1)S(1)}, bf16[1,256,256]{2,1,0:T(8,128)(2,1)S(1)}, u32[]{:S(2)}, u32[]{:S(2)}) collective-permute-start(bf16[1,256,256]{2,1,0:T(8,128)(2,1)S(1)} %get-tuple-element.49), channel_id=1, source_target_pairs={{0,2},{1,3},{2,0},{3,1},{4,6},{5,7},{6,4},{7,5},{8,10},{9,11},{10,... | collective-permute-start | bytes 393224 | tf_op jit(solution)/shard_map/ppermute | solution.py:173
  38.5 1.2 %collective-permute-done.18.refs_1_ = bf16[1,256,256]{2,1,0:T(8,128)(2,1)S(1)} collective-permute-done((bf16[1,256,256]{2,1,0:T(8,128)(2,1)S(1)}, bf16[1,256,256]{2,1,0:T(8,128)(2,1)S(1)}, u32[]{:S(2)}, u32[]{:S(2)}) %collective-permute-start.18) | collective-permute-done | bytes 131104 | tf_op jit(solution)/shard_map/ppermute | solution.py:173
  39.7 3.7 %collective-permute-start.21 = (bf16[256,256]{1,0:T(8,128)(2,1)S(1)}, bf16[256,256]{1,0:T(8,128)(2,1)S(1)}, u32[]{:S(2)}, u32[]{:S(2)}) collective-permute-start(bf16[256,256]{1,0:T(8,128)(2,1)S(1)} %shard_map.109), channel_id=1, source_target_pairs={{0,8},{1,9},{2,10},{3,11},{4,12},{5,13},{6,14},{7,15},{8,0},{9,1},... | collective-permute-start | bytes 393224 | tf_op jit(solution)/shard_map/ppermute | solution.py:173
  43.4 0.5 collective-permute-start.19
  43.9 0.9 %collective-permute-done.26.refs_2_ = bf16[144,256]{1,0:T(8,128)(2,1)S(1)} collective-permute-done((bf16[144,256]{1,0:T(8,128)(2,1)S(1)}, bf16[144,256]{1,0:T(8,128)(2,1)S(1)}, u32[]{:S(2)}, u32[]{:S(2)}) %collective-permute-start.26) | collective-permute-done | bytes 73760 | tf_op jit(solution)/shard_map/ppermute | solution.py:173
  44.9 0.6 %collective-permute-start.28 = (bf16[144,256]{1,0:T(8,128)(2,1)S(1)}, bf16[144,256]{1,0:T(8,128)(2,1)S(1)}, u32[]{:S(2)}, u32[]{:S(2)}) collective-permute-start(bf16[144,256]{1,0:T(8,128)(2,1)S(1)} %shard_map.113.refs_0_), channel_id=1, source_target_pairs={{0,2},{1,3},{2,0},{3,1},{4,6},{5,7},{6,4},{7,5},{8,10},{9,11},{10,... | collective-permute-start | bytes 221192 | tf_op jit(solution)/shard_map/ppermute | solution.py:173
  45.5 1.5 %collective-permute-start.17 = (bf16[1,256,256]{2,1,0:T(8,128)(2,1)S(1)}, bf16[1,256,256]{2,1,0:T(8,128)(2,1)S(1)}, u32[]{:S(2)}, u32[]{:S(2)}) collective-permute-start(bf16[1,256,256]{2,1,0:T(8,128)(2,1)S(1)} %get-tuple-element.43), channel_id=1, source_target_pairs={{0,2},{1,3},{2,0},{3,1},{4,6},{5,7},{6,4},{7,5},{8,10},{9,11},{10,... | collective-permute-start | bytes 393224 | tf_op jit(solution)/shard_map/ppermute | solution.py:173
  47.1 2.2 %collective-permute-done.28.refs_1_ = bf16[144,256]{1,0:T(8,128)(2,1)S(1)} collective-permute-done((bf16[144,256]{1,0:T(8,128)(2,1)S(1)}, bf16[144,256]{1,0:T(8,128)(2,1)S(1)}, u32[]{:S(2)}, u32[]{:S(2)}) %collective-permute-start.28) | collective-permute-done | bytes 73760 | tf_op jit(solution)/shard_map/ppermute | solution.py:173
  49.3 2.8 %collective-permute-done.21.refs_3_.refs_1_ = bf16[256,256]{1,0:T(8,128)(2,1)S(1)} collective-permute-done((bf16[256,256]{1,0:T(8,128)(2,1)S(1)}, bf16[256,256]{1,0:T(8,128)(2,1)S(1)}, u32[]{:S(2)}, u32[]{:S(2)}) %collective-permute-start.21) | collective-permute-done | bytes 131104 | tf_op jit(solution)/shard_map/ppermute | solution.py:173
  52.1 0.1 collective-permute-start.29
  52.2 2.0 %collective-permute-done.23.refs_2_ = bf16[256,256]{1,0:T(8,128)(2,1)S(1)} collective-permute-done((bf16[256,256]{1,0:T(8,128)(2,1)S(1)}, bf16[256,256]{1,0:T(8,128)(2,1)S(1)}, u32[]{:S(2)}, u32[]{:S(2)}) %collective-permute-start.23) | collective-permute-done | bytes 131104 | tf_op jit(solution)/shard_map/ppermute | solution.py:173
  54.2 0.9 %shard_map.115 = (bf16[256,256]{1,0:T(8,128)(2,1)}, f32[256,256]{1,0:T(8,128)}, f32[1,256]{1,0:T(1,128)}) custom-call(s32[1]{0:T(128)} %bitcast.3.core, f32[256,256]{1,0:T(8,128)S(1)} %shard_map.107.kept, bf16[256,256]{1,0:T(8,128)(2,1)S(1)} %collective-permute-done.19.refs_2_.refs_0_, bf16[256,256]{1,0:T(8,128)(2,1)S(1)} %collective-permute-done.21.refs_3_.refs_1_, ...), custom_call_target="tpu_custom_call" | custom-call | flops 33554432 | bytes 1048576 | tf_op jit(solution)/shard_map/pallas_call | solution.py:34
  (39 shorter events, 0.3 us)
Async XLA Ops:
  0.6 14.3 %collective-permute-start.11 = (bf16[256,256]{1,0:T(8,128)(2,1)}, bf16[256,256]{1,0:T(8,128)(2,1)S(1)}, u32[]{:S(2)}, u32[]{:S(2)}) collective-permute-start(bf16[256,256]{1,0:T(8,128)(2,1)} %refs_8_.1), channel_id=1, source_target_pairs={{0,8},{1,9},{2,10},{3,11},{4,12},{5,13},{6,14},{7,15},{8,0},{9,1},... | collective-permute-start | bytes 393224 | tf_op jit(solution)/shard_map/ppermute | solution.py:173
  4.7 10.7 %collective-permute-start.9 = (bf16[256,256]{1,0:T(8,128)(2,1)}, bf16[256,256]{1,0:T(8,128)(2,1)S(1)}, u32[]{:S(2)}, u32[]{:S(2)}) collective-permute-start(bf16[256,256]{1,0:T(8,128)(2,1)} %refs_8_.1), channel_id=1, source_target_pairs={{0,4},{1,5},{2,6},{3,7},{4,0},{5,1},{6,2},{7,3},{8,12},{9,13},{10,... | collective-permute-start | bytes 393224 | tf_op jit(solution)/shard_map/ppermute | solution.py:173
  6.3 9.2 %collective-permute-start.8 = (bf16[256,256]{1,0:T(8,128)(2,1)}, bf16[256,256]{1,0:T(8,128)(2,1)S(1)}, u32[]{:S(2)}, u32[]{:S(2)}) collective-permute-start(bf16[256,256]{1,0:T(8,128)(2,1)} %refs_8_.1), channel_id=1, source_target_pairs={{0,2},{1,3},{2,0},{3,1},{4,6},{5,7},{6,4},{7,5},{8,10},{9,11},{10,... | collective-permute-start | bytes 393224 | tf_op jit(solution)/shard_map/ppermute | solution.py:173
  7.8 8.1 %collective-permute-start.13 = (bf16[256,256]{1,0:T(8,128)(2,1)}, bf16[256,256]{1,0:T(8,128)(2,1)S(1)}, u32[]{:S(2)}, u32[]{:S(2)}) collective-permute-start(bf16[256,256]{1,0:T(8,128)(2,1)} %refs_8_.1), channel_id=1, source_target_pairs={{0,12},{1,13},{2,14},{3,15},{4,8},{5,9},{6,10},{7,11},{8,4},{9,5},... | collective-permute-start | bytes 393224 | tf_op jit(solution)/shard_map/ppermute | solution.py:173
  8.7 3.4 %copy-start = (bf16[64,256,256]{2,1,0:T(8,128)(2,1)S(1)}, bf16[64,256,256]{2,1,0:T(8,128)(2,1)}, u32[]{:S(2)}) copy-start(bf16[64,256,256]{2,1,0:T(8,128)(2,1)} %tiles.3) | copy-start | bytes 25165828
  12.1 0.7 %copy-start.4 = (s32[1,64]{1,0:T(1,128)S(1)}, s32[1,64]{1,0:T(1,128)}, u32[]{:S(2)}) copy-start(s32[1,64]{1,0:T(1,128)} %param.11) | copy-start | bytes 772
  12.7 12.8 %copy-start.2 = (bf16[256,256]{1,0:T(8,128)(2,1)S(1)}, bf16[256,256]{1,0:T(8,128)(2,1)}, u32[]{:S(2)}) copy-start(bf16[256,256]{1,0:T(8,128)(2,1)} %refs_8_.1) | copy-start | bytes 393220
  14.8 13.0 %copy-start.1 = (bf16[256,256]{1,0:T(8,128)(2,1)S(1)}, bf16[256,256]{1,0:T(8,128)(2,1)}, u32[]{:S(2)}) copy-start(bf16[256,256]{1,0:T(8,128)(2,1)} %refs_3_.1) | copy-start | bytes 393220
  14.8 13.0 %copy-start.3 = (bf16[256,256]{1,0:T(8,128)(2,1)S(1)}, bf16[256,256]{1,0:T(8,128)(2,1)}, u32[]{:S(2)}) copy-start(bf16[256,256]{1,0:T(8,128)(2,1)} %cotangent.1) | copy-start | bytes 393220
  14.8 13.0 %copy-start.5 = (f32[256]{0:T(256)S(1)}, f32[256]{0:T(256)}, u32[]{:S(2)}) copy-start(f32[256]{0:T(256)} %param.9) | copy-start | bytes 3076
  14.8 1.4 %collective-permute-start = (bf16[1,256,256]{2,1,0:T(8,128)(2,1)S(1)}, bf16[1,256,256]{2,1,0:T(8,128)(2,1)S(1)}, u32[]{:S(2)}, u32[]{:S(2)}) collective-permute-start(bf16[1,256,256]{2,1,0:T(8,128)(2,1)S(1)} %get-tuple-element.30), channel_id=1, source_target_pairs={{0,1},{1,0},{2,3},{3,2},{4,5},{5,4},{6,7},{7,6},{8,9},{9,8},{10,11... | collective-permute-start | bytes 393224 | tf_op jit(solution)/shard_map/ppermute | solution.py:173
  14.9 1.5 %collective-permute-start.1 = (bf16[1,256,256]{2,1,0:T(8,128)(2,1)S(1)}, bf16[1,256,256]{2,1,0:T(8,128)(2,1)S(1)}, u32[]{:S(2)}, u32[]{:S(2)}) collective-permute-start(bf16[1,256,256]{2,1,0:T(8,128)(2,1)S(1)} %get-tuple-element.31), channel_id=1, source_target_pairs={{0,1},{1,0},{2,3},{3,2},{4,5},{5,4},{6,7},{7,6},{8,9},{9,8},{10,11... | collective-permute-start | bytes 393224 | tf_op jit(solution)/shard_map/ppermute | solution.py:173
  15.4 1.3 %collective-permute-start.2 = (bf16[1,256,256]{2,1,0:T(8,128)(2,1)S(1)}, bf16[1,256,256]{2,1,0:T(8,128)(2,1)S(1)}, u32[]{:S(2)}, u32[]{:S(2)}) collective-permute-start(bf16[1,256,256]{2,1,0:T(8,128)(2,1)S(1)} %get-tuple-element.32), channel_id=1, source_target_pairs={{0,1},{1,0},{2,3},{3,2},{4,5},{5,4},{6,7},{7,6},{8,9},{9,8},{10,11... | collective-permute-start | bytes 393224 | tf_op jit(solution)/shard_map/ppermute | solution.py:173
  15.5 1.5 %collective-permute-start.3 = (bf16[1,256,256]{2,1,0:T(8,128)(2,1)S(1)}, bf16[1,256,256]{2,1,0:T(8,128)(2,1)S(1)}, u32[]{:S(2)}, u32[]{:S(2)}) collective-permute-start(bf16[1,256,256]{2,1,0:T(8,128)(2,1)S(1)} %get-tuple-element.33), channel_id=1, source_target_pairs={{0,1},{1,0},{2,3},{3,2},{4,5},{5,4},{6,7},{7,6},{8,9},{9,8},{10,11... | collective-permute-start | bytes 393224 | tf_op jit(solution)/shard_map/ppermute | solution.py:173
  15.9 1.9 %collective-permute-start.4 = (bf16[1,256,256]{2,1,0:T(8,128)(2,1)S(1)}, bf16[1,256,256]{2,1,0:T(8,128)(2,1)S(1)}, u32[]{:S(2)}, u32[]{:S(2)}) collective-permute-start(bf16[1,256,256]{2,1,0:T(8,128)(2,1)S(1)} %get-tuple-element.34), channel_id=1, source_target_pairs={{0,1},{1,0},{2,3},{3,2},{4,5},{5,4},{6,7},{7,6},{8,9},{9,8},{10,11... | collective-permute-start | bytes 393224 | tf_op jit(solution)/shard_map/ppermute | solution.py:173
  16.3 4.0 %collective-permute-start.5 = (bf16[1,256,256]{2,1,0:T(8,128)(2,1)S(1)}, bf16[1,256,256]{2,1,0:T(8,128)(2,1)S(1)}, u32[]{:S(2)}, u32[]{:S(2)}) collective-permute-start(bf16[1,256,256]{2,1,0:T(8,128)(2,1)S(1)} %get-tuple-element.35), channel_id=1, source_target_pairs={{0,1},{1,0},{2,3},{3,2},{4,5},{5,4},{6,7},{7,6},{8,9},{9,8},{10,11... | collective-permute-start | bytes 393224 | tf_op jit(solution)/shard_map/ppermute | solution.py:173
  16.5 6.5 %collective-permute-start.6 = (bf16[1,256,256]{2,1,0:T(8,128)(2,1)S(1)}, bf16[1,256,256]{2,1,0:T(8,128)(2,1)S(1)}, u32[]{:S(2)}, u32[]{:S(2)}) collective-permute-start(bf16[1,256,256]{2,1,0:T(8,128)(2,1)S(1)} %get-tuple-element.36), channel_id=1, source_target_pairs={{0,1},{1,0},{2,3},{3,2},{4,5},{5,4},{6,7},{7,6},{8,9},{9,8},{10,11... | collective-permute-start | bytes 393224 | tf_op jit(solution)/shard_map/ppermute | solution.py:173
  16.8 6.2 %collective-permute-start.7 = (bf16[1,256,256]{2,1,0:T(8,128)(2,1)S(1)}, bf16[1,256,256]{2,1,0:T(8,128)(2,1)S(1)}, u32[]{:S(2)}, u32[]{:S(2)}) collective-permute-start(bf16[1,256,256]{2,1,0:T(8,128)(2,1)S(1)} %get-tuple-element.37), channel_id=1, source_target_pairs={{0,1},{1,0},{2,3},{3,2},{4,5},{5,4},{6,7},{7,6},{8,9},{9,8},{10,11... | collective-permute-start | bytes 393224 | tf_op jit(solution)/shard_map/ppermute | solution.py:173
  17.0 6.0 %collective-permute-start.12 = (bf16[256,256]{1,0:T(8,128)(2,1)S(1)}, bf16[256,256]{1,0:T(8,128)(2,1)S(1)}, u32[]{:S(2)}, u32[]{:S(2)}) collective-permute-start(bf16[256,256]{1,0:T(8,128)(2,1)S(1)} %collective-permute-done.11.refs_12_), channel_id=1, source_target_pairs={{0,2},{1,3},{2,0},{3,1},{4,6},{5,7},{6,4},{7,5},{8,10},{9,11},{10,... | collective-permute-start | bytes 393224 | tf_op jit(solution)/shard_map/ppermute | solution.py:173
  17.8 5.9 %collective-permute-start.10 = (bf16[256,256]{1,0:T(8,128)(2,1)S(1)}, bf16[256,256]{1,0:T(8,128)(2,1)S(1)}, u32[]{:S(2)}, u32[]{:S(2)}) collective-permute-start(bf16[256,256]{1,0:T(8,128)(2,1)S(1)} %collective-permute-done.8.refs_9_), channel_id=1, source_target_pairs={{0,4},{1,5},{2,6},{3,7},{4,0},{5,1},{6,2},{7,3},{8,12},{9,13},{10,... | collective-permute-start | bytes 393224 | tf_op jit(solution)/shard_map/ppermute | solution.py:173
  20.3 5.2 %collective-permute-start.14 = (bf16[256,256]{1,0:T(8,128)(2,1)S(1)}, bf16[256,256]{1,0:T(8,128)(2,1)S(1)}, u32[]{:S(2)}, u32[]{:S(2)}) collective-permute-start(bf16[256,256]{1,0:T(8,128)(2,1)S(1)} %collective-permute-done.13.refs_14_), channel_id=1, source_target_pairs={{0,2},{1,3},{2,0},{3,1},{4,6},{5,7},{6,4},{7,5},{8,10},{9,11},{10,... | collective-permute-start | bytes 393224 | tf_op jit(solution)/shard_map/ppermute | solution.py:173
  26.2 1.6 %collective-permute-start.15 = (f32[256,256]{1,0:T(8,128)S(1)}, f32[256,256]{1,0:T(8,128)S(1)}, u32[]{:S(2)}, u32[]{:S(2)}) collective-permute-start(f32[256,256]{1,0:T(8,128)S(1)} %get-tuple-element.39), channel_id=1, source_target_pairs={{0,1},{1,0},{2,3},{3,2},{4,5},{5,4},{6,7},{7,6},{8,9},{9,8},{10,11... | collective-permute-start | bytes 786440 | tf_op jit(solution)/shard_map/ppermute | solution.py:173
  28.8 1.3 %collective-permute-start.16 = (bf16[256,256]{1,0:T(8,128)(2,1)S(1)}, bf16[256,256]{1,0:T(8,128)(2,1)S(1)}, u32[]{:S(2)}, u32[]{:S(2)}) collective-permute-start(bf16[256,256]{1,0:T(8,128)(2,1)S(1)} %get-tuple-element.41.grad), channel_id=1, source_target_pairs={{0,1},{1,0},{2,3},{3,2},{4,5},{5,4},{6,7},{7,6},{8,9},{9,8},{10,11... | collective-permute-start | bytes 393224 | tf_op jit(solution)/shard_map/ppermute | solution.py:173
  29.2 3.7 %collective-permute-start.24 = (f32[144,256]{1,0:T(8,128)S(1)}, f32[144,256]{1,0:T(8,128)S(1)}, u32[]{:S(2)}, u32[]{:S(2)}) collective-permute-start(f32[144,256]{1,0:T(8,128)S(1)} %get-tuple-element.52), channel_id=1, source_target_pairs={{0,1},{1,0},{2,3},{3,2},{4,5},{5,4},{6,7},{7,6},{8,9},{9,8},{10,11... | collective-permute-start | bytes 442376 | tf_op jit(solution)/shard_map/ppermute | solution.py:173
  30.8 6.6 %collective-permute-start.20 = (bf16[1,256,256]{2,1,0:T(8,128)(2,1)S(1)}, bf16[1,256,256]{2,1,0:T(8,128)(2,1)S(1)}, u32[]{:S(2)}, u32[]{:S(2)}) collective-permute-start(bf16[1,256,256]{2,1,0:T(8,128)(2,1)S(1)} %get-tuple-element.47), channel_id=1, source_target_pairs={{0,2},{1,3},{2,0},{3,1},{4,6},{5,7},{6,4},{7,5},{8,10},{9,11},{10,... | collective-permute-start | bytes 393224 | tf_op jit(solution)/shard_map/ppermute | solution.py:173
  31.5 8.2 %collective-permute-start.18 = (bf16[1,256,256]{2,1,0:T(8,128)(2,1)S(1)}, bf16[1,256,256]{2,1,0:T(8,128)(2,1)S(1)}, u32[]{:S(2)}, u32[]{:S(2)}) collective-permute-start(bf16[1,256,256]{2,1,0:T(8,128)(2,1)S(1)} %get-tuple-element.45.refs_2_), channel_id=1, source_target_pairs={{0,2},{1,3},{2,0},{3,1},{4,6},{5,7},{6,4},{7,5},{8,10},{9,11},{10,... | collective-permute-start | bytes 393224 | tf_op jit(solution)/shard_map/ppermute | solution.py:173
  33.0 10.5 %collective-permute-start.27 = (bf16[144,256]{1,0:T(8,128)(2,1)S(1)}, bf16[144,256]{1,0:T(8,128)(2,1)S(1)}, u32[]{:S(2)}, u32[]{:S(2)}) collective-permute-start(bf16[144,256]{1,0:T(8,128)(2,1)S(1)} %shard_map.112.refs_0_), channel_id=1, source_target_pairs={{0,12},{1,13},{2,14},{3,15},{4,8},{5,9},{6,10},{7,11},{8,4},{9,5},... | collective-permute-start | bytes 221192 | tf_op jit(solution)/shard_map/ppermute | solution.py:173
  36.0 8.8 %collective-permute-start.26 = (bf16[144,256]{1,0:T(8,128)(2,1)S(1)}, bf16[144,256]{1,0:T(8,128)(2,1)S(1)}, u32[]{:S(2)}, u32[]{:S(2)}) collective-permute-start(bf16[144,256]{1,0:T(8,128)(2,1)S(1)} %shard_map.112.refs_0_), channel_id=1, source_target_pairs={{0,8},{1,9},{2,10},{3,11},{4,12},{5,13},{6,14},{7,15},{8,0},{9,1},... | collective-permute-start | bytes 221192 | tf_op jit(solution)/shard_map/ppermute | solution.py:173
  36.4 8.4 %collective-permute-start.25 = (bf16[144,256]{1,0:T(8,128)(2,1)S(1)}, bf16[144,256]{1,0:T(8,128)(2,1)S(1)}, u32[]{:S(2)}, u32[]{:S(2)}) collective-permute-start(bf16[144,256]{1,0:T(8,128)(2,1)S(1)} %shard_map.112.refs_0_), channel_id=1, source_target_pairs={{0,4},{1,5},{2,6},{3,7},{4,0},{5,1},{6,2},{7,3},{8,12},{9,13},{10,... | collective-permute-start | bytes 221192 | tf_op jit(solution)/shard_map/ppermute | solution.py:173
  37.4 9.6 %collective-permute-start.22 = (bf16[1,256,256]{2,1,0:T(8,128)(2,1)S(1)}, bf16[1,256,256]{2,1,0:T(8,128)(2,1)S(1)}, u32[]{:S(2)}, u32[]{:S(2)}) collective-permute-start(bf16[1,256,256]{2,1,0:T(8,128)(2,1)S(1)} %get-tuple-element.49), channel_id=1, source_target_pairs={{0,2},{1,3},{2,0},{3,1},{4,6},{5,7},{6,4},{7,5},{8,10},{9,11},{10,... | collective-permute-start | bytes 393224 | tf_op jit(solution)/shard_map/ppermute | solution.py:173
  39.7 12.3 %collective-permute-start.21 = (bf16[256,256]{1,0:T(8,128)(2,1)S(1)}, bf16[256,256]{1,0:T(8,128)(2,1)S(1)}, u32[]{:S(2)}, u32[]{:S(2)}) collective-permute-start(bf16[256,256]{1,0:T(8,128)(2,1)S(1)} %shard_map.109), channel_id=1, source_target_pairs={{0,8},{1,9},{2,10},{3,11},{4,12},{5,13},{6,14},{7,15},{8,0},{9,1},... | collective-permute-start | bytes 393224 | tf_op jit(solution)/shard_map/ppermute | solution.py:173
  43.4 8.6 %collective-permute-start.19 = (bf16[256,256]{1,0:T(8,128)(2,1)S(1)}, bf16[256,256]{1,0:T(8,128)(2,1)S(1)}, u32[]{:S(2)}, u32[]{:S(2)}) collective-permute-start(bf16[256,256]{1,0:T(8,128)(2,1)S(1)} %shard_map.108), channel_id=1, source_target_pairs={{0,12},{1,13},{2,14},{3,15},{4,8},{5,9},{6,10},{7,11},{8,4},{9,5},... | collective-permute-start | bytes 393224 | tf_op jit(solution)/shard_map/ppermute | solution.py:173
  44.9 4.4 %collective-permute-start.28 = (bf16[144,256]{1,0:T(8,128)(2,1)S(1)}, bf16[144,256]{1,0:T(8,128)(2,1)S(1)}, u32[]{:S(2)}, u32[]{:S(2)}) collective-permute-start(bf16[144,256]{1,0:T(8,128)(2,1)S(1)} %shard_map.113.refs_0_), channel_id=1, source_target_pairs={{0,2},{1,3},{2,0},{3,1},{4,6},{5,7},{6,4},{7,5},{8,10},{9,11},{10,... | collective-permute-start | bytes 221192 | tf_op jit(solution)/shard_map/ppermute | solution.py:173
  45.5 6.7 %collective-permute-start.17 = (bf16[1,256,256]{2,1,0:T(8,128)(2,1)S(1)}, bf16[1,256,256]{2,1,0:T(8,128)(2,1)S(1)}, u32[]{:S(2)}, u32[]{:S(2)}) collective-permute-start(bf16[1,256,256]{2,1,0:T(8,128)(2,1)S(1)} %get-tuple-element.43), channel_id=1, source_target_pairs={{0,2},{1,3},{2,0},{3,1},{4,6},{5,7},{6,4},{7,5},{8,10},{9,11},{10,... | collective-permute-start | bytes 393224 | tf_op jit(solution)/shard_map/ppermute | solution.py:173
  47.0 7.2 %collective-permute-start.23 = (bf16[256,256]{1,0:T(8,128)(2,1)S(1)}, bf16[256,256]{1,0:T(8,128)(2,1)S(1)}, u32[]{:S(2)}, u32[]{:S(2)}) collective-permute-start(bf16[256,256]{1,0:T(8,128)(2,1)S(1)} %shard_map.110), channel_id=1, source_target_pairs={{0,4},{1,5},{2,6},{3,7},{4,0},{5,1},{6,2},{7,3},{8,12},{9,13},{10,... | collective-permute-start | bytes 393224 | tf_op jit(solution)/shard_map/ppermute | solution.py:173
  52.1 2.1 %collective-permute-start.29 = (f32[128,256]{1,0:T(8,128)S(1)}, f32[128,256]{1,0:T(8,128)S(1)}, u32[]{:S(2)}, u32[]{:S(2)}) collective-permute-start(f32[128,256]{1,0:T(8,128)S(1)} %slice.4), channel_id=1, source_target_pairs={{0,1},{1,0},{2,3},{3,2},{4,5},{5,4},{6,7},{7,6},{8,9},{9,8},{10,11... | collective-permute-start | bytes 393224 | tf_op jit(solution)/shard_map/ppermute | solution.py:173
